TPU v7x, 128 devices: a whole 4x4x4 slice. The times are simulated.
128 devices in a mesh: img: 8 (over z_lo, x), cls: 16 (over z_hi, y, core).
Axes of the slice: x: 4, y: 4, z: 4 (z_hi: 2, z_lo: 2; z = z_hi * 2 + z_lo), core: 2. Of those that a mesh axis runs over, the one named last changes fastest.
Arguments:
- spectra: bfloat16 [32768, 64, 256], P(('img', 'cls')), may hold values from -40 to 40
- offsets: int32 [32768, 2], P(('img', 'cls')), may hold values from -6 to 6
- groups: int32 [32768], P(('img', 'cls')), may hold values from 0 to 31
- ctf: float32 [32, 64], replicated, may hold values from -1 to 1
- noise_weight: float32 [64], replicated, may hold values from 0.008 to 0.08
- references: bfloat16 [256, 16384], P('cls'), may hold values from -5 to 5
Outputs:
- class_sums: float32 [256, 16384], P('cls', 'img')
- max_prob: float32 [32768], P(('img', 'cls'))
All inputs are finite; a program needn't handle non-finite values.
Results may differ from a plain program's by a relative error of at most 0.019.
Values may be sent and summed in bfloat16 or wider, within the bound.
A program may use at most 128 MiB of HBM per device.

v0:
```python
import math

import jax
import jax.numpy as jnp
from jax import lax
from jax.sharding import PartitionSpec as P

ROTS = 16


def shifted(x, axis, by):
    devices = lax.axis_size(axis)
    return lax.ppermute(x, axis, [(i, (i + by) % devices) for i in range(devices)])


def rotation_table():
    idx = jnp.arange(ROTS, dtype=jnp.float32)
    angle = 2.0 * math.pi * idx[:, None] * idx[None, :] / ROTS
    return jnp.stack([jnp.cos(angle), jnp.sin(angle)], axis=0)


def back_table():
    idx = jnp.arange(ROTS, dtype=jnp.float32)
    angle = 2.0 * math.pi * idx[:, None] * idx[None, :] / ROTS
    return jnp.stack([jnp.cos(angle), jnp.sin(angle)], axis=1)


def harmonic_table(angles):
    quarter = angles // ROTS
    samples = jnp.arange(angles, dtype=jnp.int32)
    orders = (
        ROTS * jnp.arange(quarter, dtype=jnp.int32)[None, :]
        + jnp.arange(ROTS, dtype=jnp.int32)[:, None]
    )
    turns = samples[:, None, None] * orders[None, :, :] % angles
    angle = 2.0 * math.pi * turns.astype(jnp.float32) / angles
    cosine = jnp.cos(angle)
    sine = jnp.sin(angle)
    upper = jnp.stack([cosine, -sine], axis=2)
    lower = jnp.stack([sine, cosine], axis=2)
    return jnp.concatenate([upper, lower], axis=0) / math.sqrt(angles)


def prepare(spectra, offsets, groups, ctf, noise_weight):
    count, cycles, double = spectra.shape
    angles = double // 2
    values = spectra.astype(jnp.float32)
    real_part = values[:, :, :angles]
    imag_part = values[:, :, angles:]
    theta = 2.0 * math.pi * jnp.arange(angles, dtype=jnp.float32) / angles
    radius = jnp.arange(cycles, dtype=jnp.float32) + 1.0
    shift_x = offsets[:, 0].astype(jnp.float32)
    shift_y = offsets[:, 1].astype(jnp.float32)
    along = (
        jnp.cos(theta)[None, None, :] * shift_x[:, None, None]
        + jnp.sin(theta)[None, None, :] * shift_y[:, None, None]
    )
    phase = -2.0 * math.pi * radius[None, :, None] * along / (2.0 * cycles)
    onehot = (groups[:, None] == jnp.arange(ctf.shape[0], dtype=jnp.int32)[None, :]).astype(
        jnp.float32
    )
    contrast = jnp.dot(onehot, ctf, precision=lax.Precision.HIGHEST)
    cosine = jnp.cos(phase)
    sine = jnp.sin(phase)
    shifted_re = contrast[:, :, None] * (real_part * cosine - imag_part * sine)
    shifted_im = contrast[:, :, None] * (real_part * sine + imag_part * cosine)
    merged = jnp.concatenate([shifted_re, shifted_im], axis=-1)
    harm = jnp.einsum(
        "nrc,cjpq->njprq", merged, harmonic_table(angles), precision=lax.Precision.HIGHEST
    )
    harm = harm.astype(jnp.bfloat16).reshape(count, ROTS, 2 * cycles * (angles // ROTS))
    weights = noise_weight[None, :] * contrast * contrast
    return (harm, weights)


def block_scores(harm, refs, weights, noise_weight):
    count = harm.shape[0]
    blocks = refs.shape[0]
    cycles = weights.shape[1]
    inner = refs.shape[1] // (2 * ROTS)
    raw = refs.astype(jnp.float32).reshape(blocks, ROTS, 2, cycles, inner // cycles)
    energy = jnp.sum(raw * raw, axis=(1, 2, 4))
    refw = (
        (raw * noise_weight[None, None, None, :, None])
        .astype(jnp.bfloat16)
        .reshape(blocks, ROTS, 2, inner)
    )
    real_ref = refw[:, :, 0]
    imag_ref = refw[:, :, 1]
    pair = jnp.stack(
        [jnp.concatenate([real_ref, imag_ref], -1), jnp.concatenate([imag_ref, -real_ref], -1)],
        axis=2,
    )
    corr = jnp.einsum("njk,cjok->ncoj", harm, pair, preferred_element_type=jnp.float32)
    cross = jnp.einsum("ncoj,ojk->nck", corr, rotation_table(), precision=lax.Precision.HIGHEST)
    normt = jnp.dot(weights, energy.T, precision=lax.Precision.HIGHEST)
    return (cross - 0.5 * normt[:, :, None]).reshape(count, blocks * ROTS)


def block_sums(wblock, harm):
    count = harm.shape[0]
    blocks = wblock.shape[1]
    inner = harm.shape[2] // 2
    stacked = harm.reshape(count, ROTS, 2, inner)
    out = jnp.einsum("ncwj,njhk->cjwhk", wblock, stacked, preferred_element_type=jnp.float32)
    real_sum = out[:, :, 0, 0] - out[:, :, 1, 1]
    imag_sum = out[:, :, 0, 1] + out[:, :, 1, 0]
    return jnp.stack([real_sum, imag_sum], axis=2).reshape(blocks, ROTS * 2 * inner)


def on_device(spectra, offsets, groups, ctf, noise_weight, references):
    count = spectra.shape[0]
    classes_dev = references.shape[0]
    cycle_size = lax.axis_size("cls")
    classes = classes_dev * cycle_size
    mine = lax.axis_index("cls")
    harm, weights = prepare(spectra, offsets, groups, ctf, noise_weight)
    zero_index = jnp.zeros((), jnp.int32)

    def place(scores, block, first):
        fresh = block_scores(harm, block, weights, noise_weight)
        return lax.dynamic_update_slice(scores, fresh, (zero_index, first * ROTS))

    scores = jnp.zeros((count, classes * ROTS), jnp.float32)
    scores = place(scores, references, mine * classes_dev)

    def circle_step(step, carry):
        table, block = carry
        block = shifted(block, "cls", 1)
        anchor = (mine - step) % cycle_size
        return (place(table, block, anchor * classes_dev), block)

    scores, unused_block = lax.fori_loop(1, cycle_size, circle_step, (scores, references))
    top = jnp.max(scores, axis=-1, keepdims=True)
    expo = jnp.exp(scores - top)
    prob = expo / jnp.sum(expo, axis=-1, keepdims=True)
    max_prob = jnp.max(prob, axis=-1)
    wt = jnp.einsum(
        "nck,kwj->ncwj",
        prob.reshape(count, classes, ROTS),
        back_table(),
        precision=lax.Precision.HIGHEST,
    )
    wt = wt.astype(jnp.bfloat16)

    def contribution(first, rows):
        term = block_sums(lax.dynamic_slice_in_dim(wt, first, rows, 1), harm).astype(jnp.bfloat16)
        return lax.optimization_barrier(term).astype(jnp.float32)

    partial_sums = contribution((mine - 1) % cycle_size * classes_dev, classes_dev)

    def sums_step(step, running):
        running = shifted(running.astype(jnp.bfloat16), "cls", 1).astype(running.dtype)
        anchor = (mine - 1 - step) % cycle_size
        return running + contribution(anchor * classes_dev, classes_dev)

    partial_sums = lax.fori_loop(1, cycle_size, sums_step, partial_sums)
    class_sums = lax.psum_scatter(
        partial_sums.astype(jnp.bfloat16), "img", scatter_dimension=1, tiled=True
    ).astype(jnp.float32)
    return (class_sums, max_prob)


def solution(mesh):
    placed = (
        P(("img", "cls"), None, None),
        P(("img", "cls"), None),
        P(("img", "cls")),
        P(),
        P(),
        P("cls", None),
    )
    return jax.shard_map(
        on_device,
        mesh=mesh,
        in_specs=placed,
        out_specs=(P("cls", "img"), P(("img", "cls"))),
        check_vma=False,
    )
```

profile of v0, /device:TPU:0, one launch (start us, length us, event | category | flops | bytes accessed | tf_op | source)
XLA Modules:
  0.0 846.1 jit_solution(9602637139782841204)
XLA Ops:
  11.8 14.0 %copy_convert_fusion = f32[256,64,256]{2,0,1:T(8,128)} fusion(bf16[256,64,256]{2,1,0:T(8,128)(2,1)} %param.10), kind=kLoop, calls=%fused_computation.51 | loop fusion | flops 4194304 | bytes 25165824 | tf_op jit(solution)/shard_map/convert_element_type | solution.py:47
  36.1 35.1 %subtract_multiply_fusion = (f32[256,64,128]{2,0,1:T(8,128)S(1)}, f32[256,64,128]{2,0,1:T(8,128)}) fusion(f32[256,64,256]{2,0,1:T(8,128)} %copy_convert_fusion, f32[256,128]{1,0:T(8,128)S(1)} %multiply_add_fusion, f32[64]{0:T(128)S(1)} %add_multiply_fusion.1, f32[256,64]{0,1:T(8,128)S(1)} %get-tuple-element.414), kind=kLoop, calls=%fused_computation.53 | loop fusion | flops 20971520 | bytes 33751296 | tf_op jit(solution)/shard_map/mul | solution.py:65
  71.2 20.2 %fusion.39 = bf16[16,2,8,256,64]{3,2,4,1,0:T(8,128)(2,1)} fusion(f32[256,64,128]{2,0,1:T(8,128)} %get-tuple-element.399, f32[256,64,128]{2,0,1:T(8,128)S(1)} %get-tuple-element.398, f32[128,16,1,8]{0,3,2,1:T(8,128)S(1)} %get-tuple-element.406, f32[128,16,1,8]{0,3,2,1:T(8,128)S(1)} %get-tuple-element.405, f32[128,16,1,8]{0,3,2,1:T(8,128)S(1)} %get-tuple-element.404), kind=kOutput, calls=%fused_computation.57 | convolution fusion | flops 12893552640 | bytes 25362432 | tf_op jit(solution)/shard_map/nrc,cjpq->njprq/dot_general | solution.py:68
  91.4 12.5 %copy.88 = bf16[256,16,1024]{2,0,1:T(8,128)(2,1)} copy(bf16[256,16,1024]{0,2,1:T(8,128)(2,1)} %bitcast.200) | data formatting | bytes 16777216 | tf_op jit(solution)/shard_map/while | solution.py:133
  111.9 458.6 %while.32 = (s32[]{:T(128)}, f32[256,4096]{0,1:T(8,128)}, bf16[16,16384]{1,0:T(8,128)(2,1)S(1)}, f32[64]{0:T(128)S(1)}, bf16[256,16,1024]{2,0,1:T(8,128)(2,1)}, ...) while((s32[]{:T(128)}, f32[256,4096]{0,1:T(8,128)}, ...), condition=%wide.region_3.4_spmd, body=%wide.region_1.3_spmd.sunk | while | flops 300879872 | bytes 25809620 | solution.py:133
  112.2 12.5 %collective-permute-done = bf16[16,16384]{1,0:T(8,128)(2,1)S(1)} collective-permute-done((bf16[16,16384]{1,0:T(8,128)(2,1)S(1)}, bf16[16,16384]{1,0:T(8,128)(2,1)S(1)}, u32[]{:S(2)}, u32[]{:S(2)}) %collective-permute-start) | collective-permute-done | bytes 524320 | tf_op jit(solution)/shard_map/while/body/eval_jaxpr/ppermute | solution.py:13
  143.2 11.9 %collective-permute-done = bf16[16,16384]{1,0:T(8,128)(2,1)S(1)} collective-permute-done((bf16[16,16384]{1,0:T(8,128)(2,1)S(1)}, bf16[16,16384]{1,0:T(8,128)(2,1)S(1)}, u32[]{:S(2)}, u32[]{:S(2)}) %collective-permute-start) | collective-permute-done | bytes 524320 | tf_op jit(solution)/shard_map/while/body/eval_jaxpr/ppermute | solution.py:13
  173.8 11.9 %collective-permute-done = bf16[16,16384]{1,0:T(8,128)(2,1)S(1)} collective-permute-done((bf16[16,16384]{1,0:T(8,128)(2,1)S(1)}, bf16[16,16384]{1,0:T(8,128)(2,1)S(1)}, u32[]{:S(2)}, u32[]{:S(2)}) %collective-permute-start) | collective-permute-done | bytes 524320 | tf_op jit(solution)/shard_map/while/body/eval_jaxpr/ppermute | solution.py:13
  204.3 11.9 %collective-permute-done = bf16[16,16384]{1,0:T(8,128)(2,1)S(1)} collective-permute-done((bf16[16,16384]{1,0:T(8,128)(2,1)S(1)}, bf16[16,16384]{1,0:T(8,128)(2,1)S(1)}, u32[]{:S(2)}, u32[]{:S(2)}) %collective-permute-start) | collective-permute-done | bytes 524320 | tf_op jit(solution)/shard_map/while/body/eval_jaxpr/ppermute | solution.py:13
  234.9 11.9 %collective-permute-done = bf16[16,16384]{1,0:T(8,128)(2,1)S(1)} collective-permute-done((bf16[16,16384]{1,0:T(8,128)(2,1)S(1)}, bf16[16,16384]{1,0:T(8,128)(2,1)S(1)}, u32[]{:S(2)}, u32[]{:S(2)}) %collective-permute-start) | collective-permute-done | bytes 524320 | tf_op jit(solution)/shard_map/while/body/eval_jaxpr/ppermute | solution.py:13
  265.4 11.9 %collective-permute-done = bf16[16,16384]{1,0:T(8,128)(2,1)S(1)} collective-permute-done((bf16[16,16384]{1,0:T(8,128)(2,1)S(1)}, bf16[16,16384]{1,0:T(8,128)(2,1)S(1)}, u32[]{:S(2)}, u32[]{:S(2)}) %collective-permute-start) | collective-permute-done | bytes 524320 | tf_op jit(solution)/shard_map/while/body/eval_jaxpr/ppermute | solution.py:13
  295.9 11.9 %collective-permute-done = bf16[16,16384]{1,0:T(8,128)(2,1)S(1)} collective-permute-done((bf16[16,16384]{1,0:T(8,128)(2,1)S(1)}, bf16[16,16384]{1,0:T(8,128)(2,1)S(1)}, u32[]{:S(2)}, u32[]{:S(2)}) %collective-permute-start) | collective-permute-done | bytes 524320 | tf_op jit(solution)/shard_map/while/body/eval_jaxpr/ppermute | solution.py:13
  326.5 11.9 %collective-permute-done = bf16[16,16384]{1,0:T(8,128)(2,1)S(1)} collective-permute-done((bf16[16,16384]{1,0:T(8,128)(2,1)S(1)}, bf16[16,16384]{1,0:T(8,128)(2,1)S(1)}, u32[]{:S(2)}, u32[]{:S(2)}) %collective-permute-start) | collective-permute-done | bytes 524320 | tf_op jit(solution)/shard_map/while/body/eval_jaxpr/ppermute | solution.py:13
  357.0 11.9 %collective-permute-done = bf16[16,16384]{1,0:T(8,128)(2,1)S(1)} collective-permute-done((bf16[16,16384]{1,0:T(8,128)(2,1)S(1)}, bf16[16,16384]{1,0:T(8,128)(2,1)S(1)}, u32[]{:S(2)}, u32[]{:S(2)}) %collective-permute-start) | collective-permute-done | bytes 524320 | tf_op jit(solution)/shard_map/while/body/eval_jaxpr/ppermute | solution.py:13
  387.6 11.9 %collective-permute-done = bf16[16,16384]{1,0:T(8,128)(2,1)S(1)} collective-permute-done((bf16[16,16384]{1,0:T(8,128)(2,1)S(1)}, bf16[16,16384]{1,0:T(8,128)(2,1)S(1)}, u32[]{:S(2)}, u32[]{:S(2)}) %collective-permute-start) | collective-permute-done | bytes 524320 | tf_op jit(solution)/shard_map/while/body/eval_jaxpr/ppermute | solution.py:13
  418.1 11.9 %collective-permute-done = bf16[16,16384]{1,0:T(8,128)(2,1)S(1)} collective-permute-done((bf16[16,16384]{1,0:T(8,128)(2,1)S(1)}, bf16[16,16384]{1,0:T(8,128)(2,1)S(1)}, u32[]{:S(2)}, u32[]{:S(2)}) %collective-permute-start) | collective-permute-done | bytes 524320 | tf_op jit(solution)/shard_map/while/body/eval_jaxpr/ppermute | solution.py:13
  448.7 11.9 %collective-permute-done = bf16[16,16384]{1,0:T(8,128)(2,1)S(1)} collective-permute-done((bf16[16,16384]{1,0:T(8,128)(2,1)S(1)}, bf16[16,16384]{1,0:T(8,128)(2,1)S(1)}, u32[]{:S(2)}, u32[]{:S(2)}) %collective-permute-start) | collective-permute-done | bytes 524320 | tf_op jit(solution)/shard_map/while/body/eval_jaxpr/ppermute | solution.py:13
  479.2 11.9 %collective-permute-done = bf16[16,16384]{1,0:T(8,128)(2,1)S(1)} collective-permute-done((bf16[16,16384]{1,0:T(8,128)(2,1)S(1)}, bf16[16,16384]{1,0:T(8,128)(2,1)S(1)}, u32[]{:S(2)}, u32[]{:S(2)}) %collective-permute-start) | collective-permute-done | bytes 524320 | tf_op jit(solution)/shard_map/while/body/eval_jaxpr/ppermute | solution.py:13
  509.7 11.9 %collective-permute-done = bf16[16,16384]{1,0:T(8,128)(2,1)S(1)} collective-permute-done((bf16[16,16384]{1,0:T(8,128)(2,1)S(1)}, bf16[16,16384]{1,0:T(8,128)(2,1)S(1)}, u32[]{:S(2)}, u32[]{:S(2)}) %collective-permute-start) | collective-permute-done | bytes 524320 | tf_op jit(solution)/shard_map/while/body/eval_jaxpr/ppermute | solution.py:13
  540.3 11.9 %collective-permute-done = bf16[16,16384]{1,0:T(8,128)(2,1)S(1)} collective-permute-done((bf16[16,16384]{1,0:T(8,128)(2,1)S(1)}, bf16[16,16384]{1,0:T(8,128)(2,1)S(1)}, u32[]{:S(2)}, u32[]{:S(2)}) %collective-permute-start) | collective-permute-done | bytes 524320 | tf_op jit(solution)/shard_map/while/body/eval_jaxpr/ppermute | solution.py:13
  587.1 8.7 %convolution_convert_fusion = bf16[256,256,2,16]{1,3,2,0:T(8,128)(2,1)S(1)} fusion(f32[256,256,16,1]{1,2,3,0:T(8,128)} %copy.105, f32[16,1,16]{0,2,1:T(8,128)S(1)} %get-tuple-element.410, f32[16,1,16]{0,2,1:T(8,128)S(1)} %get-tuple-element.409), kind=kOutput, calls=%fused_computation.61 | convolution fusion | flops 404750848 | bytes 8390656 | tf_op jit(solution)/shard_map/nck,kwj->ncwj/dot_general | solution.py:138
  604.5 7.5 copy.96
  613.0 186.4 %while.33 = (s32[]{:T(128)}, bf16[16,16384]{1,0:T(8,128)(2,1)S(1)}, s32[]{:T(128)}, bf16[256,256,2,16]{0,1,2,3:T(8,128)(2,1)}, bf16[256,16,2,64,8]{0,4,3,2,1:T(8...) while((s32[]{:T(128)}, bf16[16,16384]{1,0:T(8,128)(2,1)S(1)}, s32[]{:T(128)}, ...), condition=%wide.region_7.8_spmd, body=%wide.region_6.7_spmd.sunk | while | flops 270270496 | bytes 20185400 | solution.py:157
  625.6 6.0 fusion.133
  650.4 6.0 fusion.133
  687.7 6.0 fusion.133
  712.6 6.0 fusion.133
  737.4 6.0 fusion.133
  762.3 6.0 fusion.133
  774.7 6.0 fusion.133
  787.1 6.0 fusion.133
  800.3 37.2 %reduce-scatter.2.cloned.1.call-done = bf16[16,2048]{1,0:T(8,128)(2,1)} async-done(((bf16[16,16384]{1,0:T(8,128)(2,1)}), bf16[16,2048]{1,0:T(8,128)(2,1)}) %reduce-scatter.2.cloned.1.call-update) | async-done | bytes 65552 | tf_op jit(solution)/shard_map/reduce_scatter | solution.py:158
  (453 shorter events, 465.5 us)
Async XLA Ops:
  7.2 830.3 %reduce-scatter.2.cloned.1.call-start = ((), (), s32[]{:S(2)}) async-start(), calls=%async_computation.1 | async-start | bytes 589824 | tf_op jit(solution)/shard_map/reduce_scatter | solution.py:158
  111.9 12.7 %collective-permute-start = (bf16[16,16384]{1,0:T(8,128)(2,1)S(1)}, bf16[16,16384]{1,0:T(8,128)(2,1)S(1)}, u32[]{:S(2)}, u32[]{:S(2)}) collective-permute-start(bf16[16,16384]{1,0:T(8,128)(2,1)S(1)} %get-tuple-element.519), channel_id=1, source_target_pairs={{0,1},{1,2},{2,3},{3,4},{4,5},{5,6},{6,7},{7,8},{8,9},{9,10},{10,1... | collective-permute-start | bytes 1572872 | tf_op jit(solution)/shard_map/while/body/eval_jaxpr/ppermute | solution.py:13
  142.9 12.3 %collective-permute-start = (bf16[16,16384]{1,0:T(8,128)(2,1)S(1)}, bf16[16,16384]{1,0:T(8,128)(2,1)S(1)}, u32[]{:S(2)}, u32[]{:S(2)}) collective-permute-start(bf16[16,16384]{1,0:T(8,128)(2,1)S(1)} %get-tuple-element.519), channel_id=1, source_target_pairs={{0,1},{1,2},{2,3},{3,4},{4,5},{5,6},{6,7},{7,8},{8,9},{9,10},{10,1... | collective-permute-start | bytes 1572872 | tf_op jit(solution)/shard_map/while/body/eval_jaxpr/ppermute | solution.py:13
  173.4 12.3 %collective-permute-start = (bf16[16,16384]{1,0:T(8,128)(2,1)S(1)}, bf16[16,16384]{1,0:T(8,128)(2,1)S(1)}, u32[]{:S(2)}, u32[]{:S(2)}) collective-permute-start(bf16[16,16384]{1,0:T(8,128)(2,1)S(1)} %get-tuple-element.519), channel_id=1, source_target_pairs={{0,1},{1,2},{2,3},{3,4},{4,5},{5,6},{6,7},{7,8},{8,9},{9,10},{10,1... | collective-permute-start | bytes 1572872 | tf_op jit(solution)/shard_map/while/body/eval_jaxpr/ppermute | solution.py:13
  204.0 12.3 %collective-permute-start = (bf16[16,16384]{1,0:T(8,128)(2,1)S(1)}, bf16[16,16384]{1,0:T(8,128)(2,1)S(1)}, u32[]{:S(2)}, u32[]{:S(2)}) collective-permute-start(bf16[16,16384]{1,0:T(8,128)(2,1)S(1)} %get-tuple-element.519), channel_id=1, source_target_pairs={{0,1},{1,2},{2,3},{3,4},{4,5},{5,6},{6,7},{7,8},{8,9},{9,10},{10,1... | collective-permute-start | bytes 1572872 | tf_op jit(solution)/shard_map/while/body/eval_jaxpr/ppermute | solution.py:13
  234.5 12.3 %collective-permute-start = (bf16[16,16384]{1,0:T(8,128)(2,1)S(1)}, bf16[16,16384]{1,0:T(8,128)(2,1)S(1)}, u32[]{:S(2)}, u32[]{:S(2)}) collective-permute-start(bf16[16,16384]{1,0:T(8,128)(2,1)S(1)} %get-tuple-element.519), channel_id=1, source_target_pairs={{0,1},{1,2},{2,3},{3,4},{4,5},{5,6},{6,7},{7,8},{8,9},{9,10},{10,1... | collective-permute-start | bytes 1572872 | tf_op jit(solution)/shard_map/while/body/eval_jaxpr/ppermute | solution.py:13
  265.0 12.3 %collective-permute-start = (bf16[16,16384]{1,0:T(8,128)(2,1)S(1)}, bf16[16,16384]{1,0:T(8,128)(2,1)S(1)}, u32[]{:S(2)}, u32[]{:S(2)}) collective-permute-start(bf16[16,16384]{1,0:T(8,128)(2,1)S(1)} %get-tuple-element.519), channel_id=1, source_target_pairs={{0,1},{1,2},{2,3},{3,4},{4,5},{5,6},{6,7},{7,8},{8,9},{9,10},{10,1... | collective-permute-start | bytes 1572872 | tf_op jit(solution)/shard_map/while/body/eval_jaxpr/ppermute | solution.py:13
  295.6 12.3 %collective-permute-start = (bf16[16,16384]{1,0:T(8,128)(2,1)S(1)}, bf16[16,16384]{1,0:T(8,128)(2,1)S(1)}, u32[]{:S(2)}, u32[]{:S(2)}) collective-permute-start(bf16[16,16384]{1,0:T(8,128)(2,1)S(1)} %get-tuple-element.519), channel_id=1, source_target_pairs={{0,1},{1,2},{2,3},{3,4},{4,5},{5,6},{6,7},{7,8},{8,9},{9,10},{10,1... | collective-permute-start | bytes 1572872 | tf_op jit(solution)/shard_map/while/body/eval_jaxpr/ppermute | solution.py:13
  326.1 12.3 %collective-permute-start = (bf16[16,16384]{1,0:T(8,128)(2,1)S(1)}, bf16[16,16384]{1,0:T(8,128)(2,1)S(1)}, u32[]{:S(2)}, u32[]{:S(2)}) collective-permute-start(bf16[16,16384]{1,0:T(8,128)(2,1)S(1)} %get-tuple-element.519), channel_id=1, source_target_pairs={{0,1},{1,2},{2,3},{3,4},{4,5},{5,6},{6,7},{7,8},{8,9},{9,10},{10,1... | collective-permute-start | bytes 1572872 | tf_op jit(solution)/shard_map/while/body/eval_jaxpr/ppermute | solution.py:13
  356.7 12.3 %collective-permute-start = (bf16[16,16384]{1,0:T(8,128)(2,1)S(1)}, bf16[16,16384]{1,0:T(8,128)(2,1)S(1)}, u32[]{:S(2)}, u32[]{:S(2)}) collective-permute-start(bf16[16,16384]{1,0:T(8,128)(2,1)S(1)} %get-tuple-element.519), channel_id=1, source_target_pairs={{0,1},{1,2},{2,3},{3,4},{4,5},{5,6},{6,7},{7,8},{8,9},{9,10},{10,1... | collective-permute-start | bytes 1572872 | tf_op jit(solution)/shard_map/while/body/eval_jaxpr/ppermute | solution.py:13
  387.2 12.3 %collective-permute-start = (bf16[16,16384]{1,0:T(8,128)(2,1)S(1)}, bf16[16,16384]{1,0:T(8,128)(2,1)S(1)}, u32[]{:S(2)}, u32[]{:S(2)}) collective-permute-start(bf16[16,16384]{1,0:T(8,128)(2,1)S(1)} %get-tuple-element.519), channel_id=1, source_target_pairs={{0,1},{1,2},{2,3},{3,4},{4,5},{5,6},{6,7},{7,8},{8,9},{9,10},{10,1... | collective-permute-start | bytes 1572872 | tf_op jit(solution)/shard_map/while/body/eval_jaxpr/ppermute | solution.py:13
  417.8 12.3 %collective-permute-start = (bf16[16,16384]{1,0:T(8,128)(2,1)S(1)}, bf16[16,16384]{1,0:T(8,128)(2,1)S(1)}, u32[]{:S(2)}, u32[]{:S(2)}) collective-permute-start(bf16[16,16384]{1,0:T(8,128)(2,1)S(1)} %get-tuple-element.519), channel_id=1, source_target_pairs={{0,1},{1,2},{2,3},{3,4},{4,5},{5,6},{6,7},{7,8},{8,9},{9,10},{10,1... | collective-permute-start | bytes 1572872 | tf_op jit(solution)/shard_map/while/body/eval_jaxpr/ppermute | solution.py:13
  448.3 12.3 %collective-permute-start = (bf16[16,16384]{1,0:T(8,128)(2,1)S(1)}, bf16[16,16384]{1,0:T(8,128)(2,1)S(1)}, u32[]{:S(2)}, u32[]{:S(2)}) collective-permute-start(bf16[16,16384]{1,0:T(8,128)(2,1)S(1)} %get-tuple-element.519), channel_id=1, source_target_pairs={{0,1},{1,2},{2,3},{3,4},{4,5},{5,6},{6,7},{7,8},{8,9},{9,10},{10,1... | collective-permute-start | bytes 1572872 | tf_op jit(solution)/shard_map/while/body/eval_jaxpr/ppermute | solution.py:13
  478.9 12.3 %collective-permute-start = (bf16[16,16384]{1,0:T(8,128)(2,1)S(1)}, bf16[16,16384]{1,0:T(8,128)(2,1)S(1)}, u32[]{:S(2)}, u32[]{:S(2)}) collective-permute-start(bf16[16,16384]{1,0:T(8,128)(2,1)S(1)} %get-tuple-element.519), channel_id=1, source_target_pairs={{0,1},{1,2},{2,3},{3,4},{4,5},{5,6},{6,7},{7,8},{8,9},{9,10},{10,1... | collective-permute-start | bytes 1572872 | tf_op jit(solution)/shard_map/while/body/eval_jaxpr/ppermute | solution.py:13
  509.4 12.3 %collective-permute-start = (bf16[16,16384]{1,0:T(8,128)(2,1)S(1)}, bf16[16,16384]{1,0:T(8,128)(2,1)S(1)}, u32[]{:S(2)}, u32[]{:S(2)}) collective-permute-start(bf16[16,16384]{1,0:T(8,128)(2,1)S(1)} %get-tuple-element.519), channel_id=1, source_target_pairs={{0,1},{1,2},{2,3},{3,4},{4,5},{5,6},{6,7},{7,8},{8,9},{9,10},{10,1... | collective-permute-start | bytes 1572872 | tf_op jit(solution)/shard_map/while/body/eval_jaxpr/ppermute | solution.py:13
  540.0 12.3 %collective-permute-start = (bf16[16,16384]{1,0:T(8,128)(2,1)S(1)}, bf16[16,16384]{1,0:T(8,128)(2,1)S(1)}, u32[]{:S(2)}, u32[]{:S(2)}) collective-permute-start(bf16[16,16384]{1,0:T(8,128)(2,1)S(1)} %get-tuple-element.519), channel_id=1, source_target_pairs={{0,1},{1,2},{2,3},{3,4},{4,5},{5,6},{6,7},{7,8},{8,9},{9,10},{10,1... | collective-permute-start | bytes 1572872 | tf_op jit(solution)/shard_map/while/body/eval_jaxpr/ppermute | solution.py:13
  613.0 12.3 %collective-permute-start.1 = (bf16[16,16384]{1,0:T(8,128)(2,1)S(1)}, bf16[16,16384]{1,0:T(8,128)(2,1)S(1)}, u32[]{:S(2)}, u32[]{:S(2)}) collective-permute-start(bf16[16,16384]{1,0:T(8,128)(2,1)S(1)} %get-tuple-element.556), channel_id=1, source_target_pairs={{0,1},{1,2},{2,3},{3,4},{4,5},{5,6},{6,7},{7,8},{8,9},{9,10},{10,1... | collective-permute-start | bytes 1572872 | tf_op jit(solution)/shard_map/while/body/eval_jaxpr/ppermute | solution.py:13
  625.5 12.3 %collective-permute-start.1 = (bf16[16,16384]{1,0:T(8,128)(2,1)S(1)}, bf16[16,16384]{1,0:T(8,128)(2,1)S(1)}, u32[]{:S(2)}, u32[]{:S(2)}) collective-permute-start(bf16[16,16384]{1,0:T(8,128)(2,1)S(1)} %get-tuple-element.556), channel_id=1, source_target_pairs={{0,1},{1,2},{2,3},{3,4},{4,5},{5,6},{6,7},{7,8},{8,9},{9,10},{10,1... | collective-permute-start | bytes 1572872 | tf_op jit(solution)/shard_map/while/body/eval_jaxpr/ppermute | solution.py:13
  637.9 12.3 %collective-permute-start.1 = (bf16[16,16384]{1,0:T(8,128)(2,1)S(1)}, bf16[16,16384]{1,0:T(8,128)(2,1)S(1)}, u32[]{:S(2)}, u32[]{:S(2)}) collective-permute-start(bf16[16,16384]{1,0:T(8,128)(2,1)S(1)} %get-tuple-element.556), channel_id=1, source_target_pairs={{0,1},{1,2},{2,3},{3,4},{4,5},{5,6},{6,7},{7,8},{8,9},{9,10},{10,1... | collective-permute-start | bytes 1572872 | tf_op jit(solution)/shard_map/while/body/eval_jaxpr/ppermute | solution.py:13
  650.3 12.3 %collective-permute-start.1 = (bf16[16,16384]{1,0:T(8,128)(2,1)S(1)}, bf16[16,16384]{1,0:T(8,128)(2,1)S(1)}, u32[]{:S(2)}, u32[]{:S(2)}) collective-permute-start(bf16[16,16384]{1,0:T(8,128)(2,1)S(1)} %get-tuple-element.556), channel_id=1, source_target_pairs={{0,1},{1,2},{2,3},{3,4},{4,5},{5,6},{6,7},{7,8},{8,9},{9,10},{10,1... | collective-permute-start | bytes 1572872 | tf_op jit(solution)/shard_map/while/body/eval_jaxpr/ppermute | solution.py:13
  662.7 12.3 %collective-permute-start.1 = (bf16[16,16384]{1,0:T(8,128)(2,1)S(1)}, bf16[16,16384]{1,0:T(8,128)(2,1)S(1)}, u32[]{:S(2)}, u32[]{:S(2)}) collective-permute-start(bf16[16,16384]{1,0:T(8,128)(2,1)S(1)} %get-tuple-element.556), channel_id=1, source_target_pairs={{0,1},{1,2},{2,3},{3,4},{4,5},{5,6},{6,7},{7,8},{8,9},{9,10},{10,1... | collective-permute-start | bytes 1572872 | tf_op jit(solution)/shard_map/while/body/eval_jaxpr/ppermute | solution.py:13
  675.2 12.3 %collective-permute-start.1 = (bf16[16,16384]{1,0:T(8,128)(2,1)S(1)}, bf16[16,16384]{1,0:T(8,128)(2,1)S(1)}, u32[]{:S(2)}, u32[]{:S(2)}) collective-permute-start(bf16[16,16384]{1,0:T(8,128)(2,1)S(1)} %get-tuple-element.556), channel_id=1, source_target_pairs={{0,1},{1,2},{2,3},{3,4},{4,5},{5,6},{6,7},{7,8},{8,9},{9,10},{10,1... | collective-permute-start | bytes 1572872 | tf_op jit(solution)/shard_map/while/body/eval_jaxpr/ppermute | solution.py:13
  687.6 12.3 %collective-permute-start.1 = (bf16[16,16384]{1,0:T(8,128)(2,1)S(1)}, bf16[16,16384]{1,0:T(8,128)(2,1)S(1)}, u32[]{:S(2)}, u32[]{:S(2)}) collective-permute-start(bf16[16,16384]{1,0:T(8,128)(2,1)S(1)} %get-tuple-element.556), channel_id=1, source_target_pairs={{0,1},{1,2},{2,3},{3,4},{4,5},{5,6},{6,7},{7,8},{8,9},{9,10},{10,1... | collective-permute-start | bytes 1572872 | tf_op jit(solution)/shard_map/while/body/eval_jaxpr/ppermute | solution.py:13
  700.0 12.3 %collective-permute-start.1 = (bf16[16,16384]{1,0:T(8,128)(2,1)S(1)}, bf16[16,16384]{1,0:T(8,128)(2,1)S(1)}, u32[]{:S(2)}, u32[]{:S(2)}) collective-permute-start(bf16[16,16384]{1,0:T(8,128)(2,1)S(1)} %get-tuple-element.556), channel_id=1, source_target_pairs={{0,1},{1,2},{2,3},{3,4},{4,5},{5,6},{6,7},{7,8},{8,9},{9,10},{10,1... | collective-permute-start | bytes 1572872 | tf_op jit(solution)/shard_map/while/body/eval_jaxpr/ppermute | solution.py:13
  712.5 12.3 %collective-permute-start.1 = (bf16[16,16384]{1,0:T(8,128)(2,1)S(1)}, bf16[16,16384]{1,0:T(8,128)(2,1)S(1)}, u32[]{:S(2)}, u32[]{:S(2)}) collective-permute-start(bf16[16,16384]{1,0:T(8,128)(2,1)S(1)} %get-tuple-element.556), channel_id=1, source_target_pairs={{0,1},{1,2},{2,3},{3,4},{4,5},{5,6},{6,7},{7,8},{8,9},{9,10},{10,1... | collective-permute-start | bytes 1572872 | tf_op jit(solution)/shard_map/while/body/eval_jaxpr/ppermute | solution.py:13
  724.9 12.3 %collective-permute-start.1 = (bf16[16,16384]{1,0:T(8,128)(2,1)S(1)}, bf16[16,16384]{1,0:T(8,128)(2,1)S(1)}, u32[]{:S(2)}, u32[]{:S(2)}) collective-permute-start(bf16[16,16384]{1,0:T(8,128)(2,1)S(1)} %get-tuple-element.556), channel_id=1, source_target_pairs={{0,1},{1,2},{2,3},{3,4},{4,5},{5,6},{6,7},{7,8},{8,9},{9,10},{10,1... | collective-permute-start | bytes 1572872 | tf_op jit(solution)/shard_map/while/body/eval_jaxpr/ppermute | solution.py:13
  737.3 12.3 %collective-permute-start.1 = (bf16[16,16384]{1,0:T(8,128)(2,1)S(1)}, bf16[16,16384]{1,0:T(8,128)(2,1)S(1)}, u32[]{:S(2)}, u32[]{:S(2)}) collective-permute-start(bf16[16,16384]{1,0:T(8,128)(2,1)S(1)} %get-tuple-element.556), channel_id=1, source_target_pairs={{0,1},{1,2},{2,3},{3,4},{4,5},{5,6},{6,7},{7,8},{8,9},{9,10},{10,1... | collective-permute-start | bytes 1572872 | tf_op jit(solution)/shard_map/while/body/eval_jaxpr/ppermute | solution.py:13
  749.7 12.3 %collective-permute-start.1 = (bf16[16,16384]{1,0:T(8,128)(2,1)S(1)}, bf16[16,16384]{1,0:T(8,128)(2,1)S(1)}, u32[]{:S(2)}, u32[]{:S(2)}) collective-permute-start(bf16[16,16384]{1,0:T(8,128)(2,1)S(1)} %get-tuple-element.556), channel_id=1, source_target_pairs={{0,1},{1,2},{2,3},{3,4},{4,5},{5,6},{6,7},{7,8},{8,9},{9,10},{10,1... | collective-permute-start | bytes 1572872 | tf_op jit(solution)/shard_map/while/body/eval_jaxpr/ppermute | solution.py:13
  762.2 12.3 %collective-permute-start.1 = (bf16[16,16384]{1,0:T(8,128)(2,1)S(1)}, bf16[16,16384]{1,0:T(8,128)(2,1)S(1)}, u32[]{:S(2)}, u32[]{:S(2)}) collective-permute-start(bf16[16,16384]{1,0:T(8,128)(2,1)S(1)} %get-tuple-element.556), channel_id=1, source_target_pairs={{0,1},{1,2},{2,3},{3,4},{4,5},{5,6},{6,7},{7,8},{8,9},{9,10},{10,1... | collective-permute-start | bytes 1572872 | tf_op jit(solution)/shard_map/while/body/eval_jaxpr/ppermute | solution.py:13
  774.6 12.3 %collective-permute-start.1 = (bf16[16,16384]{1,0:T(8,128)(2,1)S(1)}, bf16[16,16384]{1,0:T(8,128)(2,1)S(1)}, u32[]{:S(2)}, u32[]{:S(2)}) collective-permute-start(bf16[16,16384]{1,0:T(8,128)(2,1)S(1)} %get-tuple-element.556), channel_id=1, source_target_pairs={{0,1},{1,2},{2,3},{3,4},{4,5},{5,6},{6,7},{7,8},{8,9},{9,10},{10,1... | collective-permute-start | bytes 1572872 | tf_op jit(solution)/shard_map/while/body/eval_jaxpr/ppermute | solution.py:13
  787.0 12.3 %collective-permute-start.1 = (bf16[16,16384]{1,0:T(8,128)(2,1)S(1)}, bf16[16,16384]{1,0:T(8,128)(2,1)S(1)}, u32[]{:S(2)}, u32[]{:S(2)}) collective-permute-start(bf16[16,16384]{1,0:T(8,128)(2,1)S(1)} %get-tuple-element.556), channel_id=1, source_target_pairs={{0,1},{1,2},{2,3},{3,4},{4,5},{5,6},{6,7},{7,8},{8,9},{9,10},{10,1... | collective-permute-start | bytes 1572872 | tf_op jit(solution)/shard_map/while/body/eval_jaxpr/ppermute | solution.py:13
  799.4 39.6 %copy-start.1 = (f32[32,64]{1,0:T(8,128)S(1)}, f32[32,64]{1,0:T(8,128)}, u32[]{:S(2)}) copy-start(f32[32,64]{1,0:T(8,128)} %param.13) | copy-start | bytes 24580
  (6 other events, 39.6 us)
Sparse Core Ops, SparseCore 0:
  800.4 37.0 reduce-scatter.1
where the time goes:
time: 854 us; the launch traced here: 846 us
  waiting for transfers between devices  292 us (34%)
  matrix products  235 us (28%)
  local copies, waits for them, and re-layouts  153 us (18%)
  other arithmetic  147 us (17%)
  between operations  14.5 us (2%)
    ppermute x30, waiting for transfers between devices, shifted(): lax.ppermute(x, axis, [(i, (i + by) % devices) for i in range(devices)])  254 us
    dot_general x16, matrix products, block_sums(): jnp.einsum('ncwj,njhk->cjwhk', wblock, stacked, preferred_element_type=jn...  96.2 us
    dot_general x16, matrix products, block_scores(): jnp.einsum('njk,cjok->ncoj', harm, pair, preferred_element_type=jnp.float32)  94.2 us
    mul x16, local copies, waits for them, and re-layouts, block_scores(): energy = jnp.sum(raw * raw, axis=(1, 2, 4))  74.2 us
    reduce_sum x16, other arithmetic, block_scores(): energy = jnp.sum(raw * raw, axis=(1, 2, 4))  65.1 us
    reduce_scatter x1, waiting for transfers between devices, on_device(): lax.psum_scatter(partial_sums.astype(jnp.bfloat16), 'img', scatter_dimens...  37.2 us
    mul x1, other arithmetic, prepare(): shifted_re = contrast[:, :, None] * (real_part * cosine - imag_part * sine)  35.1 us
    dot_general x1, matrix products, prepare(): jnp.einsum('nrc,cjpq->njprq', merged, harmonic_table(angles), precision=l...  20.2 us
  transfers between devices with their start and end apart: 31, of which 31 were waited for; matrix products, arithmetic and copies ran while one was open for 13% of the time, Pallas kernels for 0%

commit v1 on v0

v1 whole, which is shorter than its diff:
```python
import math

import jax
import jax.numpy as jnp
import ml_dtypes
import numpy as np
from jax import lax
from jax.experimental import pallas as pl
from jax.experimental.pallas import tpu as pltpu
from jax.sharding import PartitionSpec as P

MESH = pl.DeviceIdType.MESH
F32 = jnp.float32
BF16 = jnp.bfloat16
HIGHEST = lax.Precision.HIGHEST

IMG = 256
R = 64
A = 128
ROTS = 16
SHIFTS = 13
LOW = 192
DEPTH = 384
WX, WY, WZ = 384, 256, 384

S1 = math.sqrt(0.5)
C1 = math.cos(math.pi / 8)
C3 = math.cos(3 * math.pi / 8)


def split_np(values):
    high = values.astype(np.float32).astype(ml_dtypes.bfloat16)
    low = (values - high.astype(np.float64)).astype(np.float32).astype(ml_dtypes.bfloat16)
    return high, low


def shift_table():
    theta = 2.0 * np.pi * np.arange(A) / A
    radius = np.arange(R) + 1.0
    step = np.arange(SHIFTS) - 6.0
    along = (
        np.cos(theta)[None, None, :] * step[:, None, None]
        + np.sin(theta)[None, None, :] * step[None, :, None]
    ).reshape(SHIFTS * SHIFTS, A)
    phase = -2.0 * np.pi * radius[:, None, None] * along[None] / (2.0 * R)
    both = np.concatenate([np.cos(phase), np.sin(phase)], axis=-1)
    high, low = split_np(both)
    table = np.zeros((R, DEPTH, 2 * A), ml_dtypes.bfloat16)
    table[:, : SHIFTS * SHIFTS] = high
    table[:, LOW : LOW + SHIFTS * SHIFTS] = low
    return table


def harmonic_rows():
    quarter = A // ROTS
    orders = ROTS * np.arange(quarter)[None, :] + np.arange(ROTS)[:, None]
    turns = (np.arange(A)[:, None, None] * orders[None]) % A
    angle = 2.0 * np.pi * turns / A
    upper = np.stack([np.cos(angle), -np.sin(angle)], axis=2)
    lower = np.stack([np.sin(angle), np.cos(angle)], axis=2)
    table = np.concatenate([upper, lower], axis=0) / math.sqrt(A)
    rows = np.ascontiguousarray(table.reshape(2 * A, 2 * A).T)
    high, low = split_np(rows)
    return np.concatenate([high, low, high], axis=1)


def cosine_part(a):
    p, m = a[0] + a[8], a[0] - a[8]
    t, d = a[2] + a[6], S1 * (a[2] - a[6])
    q = p + a[4]
    even = [q + t, m + d, p - a[4], m - d, q - t]
    s17, d17 = a[1] + a[7], a[1] - a[7]
    s35, d35 = a[3] + a[5], a[3] - a[5]
    odd = [s17 + s35, C1 * d17 + C3 * d35, S1 * (s17 - s35), C3 * d17 - C1 * d35]
    out = [even[k] + odd[k] for k in range(4)] + [even[4]]
    return out + [even[k] - odd[k] for k in (3, 2, 1, 0)]


def sine_part(b):
    t = S1 * (b[2] + b[6])
    even = [None, t + b[4], b[2] - b[6], t - b[4]]
    s17, d17 = b[1] + b[7], b[1] - b[7]
    s35, d35 = b[3] + b[5], b[3] - b[5]
    odd = [None, C3 * s17 + C1 * s35, S1 * (d17 + d35), C1 * s17 - C3 * s35, d17 - d35]
    out = [None] + [odd[k] + even[k] for k in (1, 2, 3)] + [odd[4]]
    return out + [odd[k] - even[k] for k in (3, 2, 1)]


def across(a, b, precision=None):
    return lax.dot_general(
        a, b, (((1,), (1,)), ((), ())), precision=precision, preferred_element_type=F32
    )


def plain(a, b, precision=None):
    return jnp.dot(a, b, precision=precision, preferred_element_type=F32)


def kernel(
    spectra, table, offsets, groups, ctf, noise, refs, harmonics,
    sums_out, prob_out,
    gx, gy, gz, cx, cy, cz, ht, qb, wb, norm, spec, tab, hot, cgt,
    rx1, ry1, rz1, rx2, ry2, rz2, rx3, ry3, rz3,
    dma, ag_s, ag_r, core_s, core_r, x1_s, x1_r, y1_s, y1_r, z1_s, z1_r, late_s, late_r,
):
    img = lax.axis_index("img")
    cls = lax.axis_index("cls")
    zl, x = img // 4, img % 4
    zh, y, e = cls // 8, (cls // 2) % 4, cls % 2
    other = 1 - e

    def device(zl_, x_, zh_, y_, e_):
        return (zl_ * 4 + x_, zh_ * 8 + y_ * 2 + e_)

    def at_x(d):
        return device(zl, (x + d) % 4, zh, y, e)

    def at_y(d):
        return device(zl, x, zh, (y + d) % 4, e)

    def flip(d):
        return (zh + d // 2) % 2, (zl + d) % 2

    def at_z(d):
        zh_, zl_ = flip(d)
        return device(zl_, x, zh_, y, e)

    def at_zy(d):
        return device((zl + 1) % 2, x, (zh + 1) % 2, (y + d) % 4, e)

    twin = device(zl, x, zh, y, other)

    def remote(src, dst, send, recv, where):
        return pltpu.make_async_remote_copy(
            src_ref=src, dst_ref=dst, send_sem=send, recv_sem=recv,
            device_id=where, device_id_type=MESH,
        )

    def spec_copy(c):
        return pltpu.make_async_copy(
            spectra.at[:, pl.ds(c * 16, 16), :], spec.at[c % 2], dma.at[c % 2]
        )

    def tab_copy(c):
        return pltpu.make_async_copy(
            table.at[pl.ds(c * 16, 16)], tab.at[c % 2], dma.at[2 + c % 2]
        )

    spec_copy(0).start()
    tab_copy(0).start()

    barrier = pltpu.get_barrier_semaphore()
    friends = [twin]
    friends += [at_x(d) for d in (1, 2, 3)]
    friends += [at_y(d) for d in (1, 2, 3)]
    friends += [at_z(d) for d in (1, 2, 3)]
    friends += [at_zy(d) for d in (1, 2, 3)]
    for friend in friends:
        pl.semaphore_signal(barrier, inc=1, device_id=friend, device_id_type=MESH)

    spread = (
        lax.broadcasted_iota(jnp.int32, (R, 512), 0)
        == lax.broadcasted_iota(jnp.int32, (R, 512), 1) // 8
    ).astype(F32)
    nw = jnp.broadcast_to(noise[...], (8, R))
    nwx = plain(nw, spread, HIGHEST)[0:1]

    def weighted(start, width, gains):
        part = refs[:, pl.ds(pl.multiple_of(start, 128), width)].astype(F32)
        return (part * gains).astype(BF16)

    gain_x = nwx[:, :384]
    gain_y = jnp.concatenate([nwx[:, 384:], nwx[:, :128]], axis=1)
    gain_z = nwx[:, 128:]
    for k in range(4):
        j = (k // 2) * 8 + x * 2 + k % 2
        gx[e, zh, y, x, k] = weighted(j * 1024, WX, gain_x)
    for k in range(8):
        j = zl * 8 + k
        gz[e, zh, y, zl, k] = weighted(j * 1024 + WX + WY, WZ, gain_z)
    for j in range(16):
        gy[e, zh, y, j] = weighted(j * 1024 + WX, WY, gain_y)
    total = jnp.zeros((16, 512), F32)
    for k in range(32):
        part = refs[:, k * 512 : (k + 1) * 512].astype(F32)
        total = total + part * part
    ctf4 = jnp.concatenate([ctf[...]] * 4, axis=0)
    by_group = plain(0.5 * noise[...] * ctf4 * ctf4, spread, HIGHEST)
    energy = across(total, by_group, HIGHEST)
    high = energy.astype(BF16).astype(F32)
    middle = (energy - high).astype(BF16).astype(F32)
    low = energy - high - middle
    lane = lax.broadcasted_iota(jnp.int32, (16, 128), 1) // 32
    packed = jnp.where(
        lane == 0, high, jnp.where(lane == 1, middle, jnp.where(lane == 2, low, 0.0))
    ).astype(BF16)
    gy[e, zh, y, 16] = jnp.concatenate([packed, packed], axis=1)

    def ag(index, piece, where):
        return remote(piece, piece, ag_s.at[index], ag_r.at[index], where)

    mine_x = gx.at[e, zh, y, x]
    pre_x = [ag(d - 1, mine_x, at_y(d)) for d in (1, 2, 3)]
    pre_x += [ag(3, mine_x, at_z(3))]
    pre_x += [ag(3 + d, mine_x, at_zy(d)) for d in (1, 2, 3)]
    pre_z = [ag(6 + d, gz.at[e, zh, y, zl], at_y(d)) for d in (1, 2, 3)]
    pre_y = [ag(10, gy.at[e, zh, y], at_z(3))]
    last_x = [ag(10 + d, gx.at[e, :, :, x], at_x(d)) for d in (1, 2, 3)]
    last_y = [ag(13 + d, gy.at[e, :, y], at_y(d)) for d in (1, 2, 3)]
    last_z = [ag(16 + d, gz.at[e, zh, :, zl], at_z(d)) for d in (1, 2, 3)]

    def piece_x(e_, d):
        return gx.at[e_, :, :, (x + d) % 4]

    def piece_y(e_, d):
        return gy.at[e_, :, (y + d) % 4]

    def piece_z(e_, d):
        zh_, zl_ = flip(d)
        return gz.at[e_, zh_, :, zl_]

    pieces = (piece_x, piece_y, piece_z)

    def share(group, d):
        return ag(20 + 4 * group + d, pieces[group](e, d), twin)

    pl.semaphore_wait(barrier, len(friends))
    for copy in pre_x + pre_y + pre_z:
        copy.start()

    index = (offsets[:, 0:1] + 6) * SHIFTS + offsets[:, 1:2] + 6
    column = lax.broadcasted_iota(jnp.int32, (IMG, DEPTH), 1)
    hot[...] = ((column == index) | (column == index + LOW)).astype(F32).astype(BF16)
    of_group = (
        lax.broadcasted_iota(jnp.int32, (32, IMG), 0) == groups[...]
    ).astype(F32)
    cgt[...] = lax.dot_general(
        ctf[...], of_group, (((0,), (0,)), ((), ())), precision=HIGHEST, preferred_element_type=F32
    )

    def prepare(c):
        slot = c % 2
        if c < 3:
            spec_copy(c + 1).start()
            tab_copy(c + 1).start()
        spec_copy(c).wait()
        tab_copy(c).wait()

        @pl.loop(0, 16)
        def widen(b):
            part = spec[slot, pl.ds(b * 16, 16)].astype(F32)
            rows = pl.ds(pl.multiple_of(b * 256, 256), 256)
            qb[rows, :] = part[:, :, :A].reshape(256, A)
            rows = pl.ds(pl.multiple_of(4096 + b * 256, 256), 256)
            qb[rows, :] = part[:, :, A:].reshape(256, A)

        @pl.loop(0, 8)
        def pairs(b):
            found = []
            for k in range(2):
                r = b * 2 + k
                turn = plain(hot[...], tab[slot, r])
                cosine, sine = turn[:, :A], turn[:, A:]
                real = qb[pl.ds(r, IMG, stride=16), :]
                imag = qb[pl.ds(4096 + r, IMG, stride=16), :]
                value = jnp.concatenate(
                    [real * cosine - imag * sine, real * sine + imag * cosine], axis=1
                )
                high = value.astype(BF16)
                low = (value - high.astype(F32)).astype(BF16)
                out = across(harmonics[...], jnp.concatenate([high, high, low], axis=1))
                out = out * cgt[pl.ds(c * 16 + r, 1), :]
                found.append(out.reshape(32, 8, IMG))
            both = jnp.concatenate(found, axis=1)
            ht[:, pl.ds(pl.multiple_of(c * 128 + b * 16, 16), 16), :] = both.astype(BF16)

    prepare(0)
    for copy in pre_x:
        copy.wait_recv()
    for copy in last_x:
        copy.start()
    for copy in pre_y + pre_z:
        copy.wait_recv()
    for copy in last_z + last_y:
        copy.start()
    for group in range(3):
        share(group, 0).start()
    prepare(1)
    prepare(2)
    prepare(3)
    for d in (1, 3, 2):
        for group, last in ((1, last_y), (0, last_x), (2, last_z)):
            last[d - 1].wait_recv()
            share(group, d if group == 2 else 4 - d).start()
    for group in range(3):
        for d in range(4):
            share(group, d).wait_recv()

    @pl.loop(0, 16)
    def correlate(j):
        jx = (j // 2) % 4
        jz = j // 8
        part_x = gx[:, :, :, jx, jz * 2 + j % 2].reshape(256, WX)
        part_y = gy[:, :, :, j].reshape(256, WY)
        part_z = gz[:, :, :, jz, j % 8].reshape(256, WZ)
        real = jnp.concatenate([part_x, part_y[:, :128]], axis=1)
        imag = jnp.concatenate([part_y[:, 128:], part_z], axis=1)
        h_re, h_im = ht[2 * j], ht[2 * j + 1]
        q_re = plain(real, h_re) + plain(imag, h_im)
        q_im = plain(imag, h_re) - plain(real, h_im)
        for t in range(2):
            base = pl.multiple_of((t * 32 + 2 * j) * 256, 256)
            qb[pl.ds(base, 256), :] = q_re[:, t * 128 : (t + 1) * 128]
            qb[pl.ds(base + 256, 256), :] = q_im[:, t * 128 : (t + 1) * 128]

    row = lax.broadcasted_iota(jnp.int32, (128, IMG), 0)
    thrice = ((row % 32 == groups[...]) & (row < 96)).astype(F32).astype(BF16)
    norms = plain(gy[:, :, :, 16].reshape(256, WY)[:, :128], thrice)
    norm[0:256, :] = norms[:, :128]
    norm[256:512, :] = norms[:, 128:]

    for t in range(2):
        def at(k, c, t=t):
            return (t * 32 + k) * 256 + c

        def scores(b, top, t=t, at=at):
            c = pl.multiple_of(b * 8, 8)
            re = [qb[pl.ds(at(2 * j, c), 8), :] for j in range(16)]
            im = [qb[pl.ds(at(2 * j + 1, c), 8), :] for j in range(16)]
            a = [re[0]] + [re[j] + re[16 - j] for j in range(1, 8)] + [re[8]]
            s = [None] + [im[j] - im[16 - j] for j in range(1, 8)]
            a[0] = a[0] - norm[pl.ds(t * 256 + c, 8), :]
            cp, sp = cosine_part(a), sine_part(s)
            out = [cp[0]] + [cp[k] + sp[k] for k in range(1, 8)] + [cp[8]]
            out += [cp[16 - k] - sp[16 - k] for k in range(9, 16)]
            for k in range(16):
                qb[pl.ds(at(k, c), 8), :] = out[k]
                top = jnp.maximum(top, out[k])
            return top

        top = lax.fori_loop(0, 32, scores, jnp.full((8, 128), -jnp.inf, F32))
        top = jnp.max(top, axis=0, keepdims=True)

        def exponents(b, total, top=top, at=at):
            c = pl.multiple_of(b * 8, 8)
            for k in range(16):
                value = jnp.exp(qb[pl.ds(at(k, c), 8), :] - top)
                qb[pl.ds(at(k, c), 8), :] = value
                total = total + value
            return total

        total = lax.fori_loop(0, 32, exponents, jnp.zeros((8, 128), F32))
        scale = 1.0 / jnp.sum(total, axis=0, keepdims=True)
        prob_out[:, t * 128 : (t + 1) * 128] = scale

        @pl.loop(0, 16)
        def back(b, t=t, at=at, scale=scale):
            c = pl.multiple_of(b * 16, 16)
            p = [qb[pl.ds(at(k, c), 16), :] * scale for k in range(16)]
            a = [p[0]] + [p[k] + p[16 - k] for k in range(1, 8)] + [p[8]]
            s = [None] + [p[k] - p[16 - k] for k in range(1, 8)]
            cp, sp = cosine_part(a), sine_part(s)
            cols = slice(t * 128, (t + 1) * 128)
            zero = jnp.zeros((16, 128), BF16)
            for j in range(9):
                re = cp[j].astype(BF16)
                wb[j, 0, pl.ds(c, 16), cols] = re
                if j in (0, 8):
                    wb[j, 1, pl.ds(c, 16), cols] = zero
                else:
                    wb[16 - j, 0, pl.ds(c, 16), cols] = re
                    wb[j, 1, pl.ds(c, 16), cols] = sp[j].astype(BF16)
                    wb[16 - j, 1, pl.ds(c, 16), cols] = (-sp[j]).astype(BF16)

    for copy in pre_x + pre_y + pre_z + last_x + last_y + last_z:
        copy.wait_send()
    for group in range(3):
        for d in range(4):
            share(group, d).wait_send()

    def target(it):
        return (x + 1 + it) % 4, (zl + 1 + it // 4) % 2

    def trade(it):
        xt, zt = target(it)
        pairs = (
            (gx.at[other, :, :, xt, pl.ds(zt * 2, 2)], cx.at[:, :, xt, pl.ds(zt * 2, 2)]),
            (gy.at[other, :, :, pl.ds(zt * 8 + xt * 2, 2)], cy.at[:, :, pl.ds(zt * 8 + xt * 2, 2)]),
            (gz.at[other, :, :, zt, pl.ds(xt * 2, 2)], cz.at[:, :, zt, pl.ds(xt * 2, 2)]),
        )
        return [
            remote(src, dst, core_s.at[k, it], core_r.at[k, it], twin)
            for k, (src, dst) in enumerate(pairs)
        ]

    def first_x(it):
        xt, zt = target(it)
        u, half = it % 4, it // 4
        return remote(
            gx.at[e, :, :, xt, pl.ds(zt * 2, 2)], rx1.at[u, zt],
            x1_s.at[u, half], x1_r.at[u, half], at_x(u + 1),
        )

    def first_y(it, d):
        xt, zt = target(it)
        return remote(
            gy.at[e, :, (y + d) % 4, pl.ds(zt * 8 + xt * 2, 2)],
            ry1.at[d - 1, :, pl.ds(zt * 8 + xt * 2, 2)],
            y1_s.at[d - 1, it], y1_r.at[d - 1, it], at_y(d),
        )

    def first_z(it, d):
        xt, zt = target(it)
        u = it % 4
        zh_, zl_ = flip(d)
        return remote(
            gz.at[e, zh_, :, zt, pl.ds(xt * 2, 2)], rz1.at[d - 1, :, pl.ds(xt * 2, 2)],
            z1_s.at[d - 1, u], z1_r.at[d - 1, u], at_z(d),
        )

    def settle(it):
        xt, zt = target(it)
        for copy in trade(it):
            copy.wait_recv()

        @pl.loop(0, 8)
        def add(s):
            h, v = s // 4, s % 4
            k = pl.ds(zt * 2, 2)
            gx[e, h, v, xt, k] = (
                gx[e, h, v, xt, k].astype(F32) + cx[h, v, xt, k].astype(F32)
            ).astype(BF16)
            k = pl.ds(zt * 8 + xt * 2, 2)
            gy[e, h, v, k] = (
                gy[e, h, v, k].astype(F32) + cy[h, v, k].astype(F32)
            ).astype(BF16)
            k = pl.ds(xt * 2, 2)
            gz[e, h, v, zt, k] = (
                gz[e, h, v, zt, k].astype(F32) + cz[h, v, zt, k].astype(F32)
            ).astype(BF16)

        @pl.when(it % 4 != 3)
        def _():
            first_x(it).start()

        @pl.when(it < 4)
        def _():
            first_z(it, 1).start()
            first_z(it, 3).start()

        @pl.when(it >= 4)
        def _():
            first_z(it, 2).start()

        for d in (1, 3, 2):
            first_y(it, d).start()

    @pl.loop(0, 8)
    def accumulate(it):
        xt, zt = target(it)
        for k in range(2):
            j = zt * 8 + xt * 2 + k
            w_re, w_im = wb[j, 0], wb[j, 1]
            w_minus = wb[(16 - j) % 16, 1]
            h_both = jnp.concatenate([ht[2 * j], ht[2 * j + 1]], axis=1)
            out_re = across(jnp.concatenate([w_re, w_minus], axis=1), h_both).astype(BF16)
            out_im = across(jnp.concatenate([w_im, w_re], axis=1), h_both).astype(BF16)
            gx[:, :, :, xt, zt * 2 + k] = out_re[:, :384].reshape(2, 2, 4, 16, WX)
            gy[:, :, :, j] = jnp.concatenate(
                [out_re[:, 384:], out_im[:, :128]], axis=1
            ).reshape(2, 2, 4, 16, WY)
            gz[:, :, :, zt, xt * 2 + k] = out_im[:, 128:].reshape(2, 2, 4, 16, WZ)
        for copy in trade(it):
            copy.start()

        @pl.when(it > 0)
        def _():
            settle(it - 1)

    settle(7)

    for half in range(2):
        for u in range(3):
            first_x(u + 4 * half).wait_recv()

    @pl.loop(0, 8)
    def add_x1(s):
        h, v = s // 4, s % 4
        acc = gx[e, h, v, x].astype(F32).reshape(2, 2, 16, WX)
        for u in range(3):
            acc = acc + rx1[u, :, h, v].astype(F32)
        gx[e, h, v, x] = acc.reshape(4, 16, WX).astype(BF16)

    def late(stage, group, d, src, dst, where):
        return remote(
            src, dst, late_s.at[stage, group, d - 1], late_r.at[stage, group, d - 1], where
        )

    def second_x(d):
        return late(0, 0, d, gx.at[e, :, (y + d) % 4, x], rx2.at[d - 1], at_y(d))

    def second_y(d):
        zh_, zl_ = flip(d)
        return late(0, 1, d, gy.at[e, zh_, y, pl.ds(zl_ * 8, 8)], ry2.at[d - 1], at_z(d))

    def second_z(d):
        return late(
            0, 2, d, gz.at[e, zh, :, zl, pl.ds(((x + d) % 4) * 2, 2)], rz2.at[d - 1], at_x(d)
        )

    def third_x(d):
        zh_, zl_ = flip(d)
        return late(1, 0, d, gx.at[e, zh_, y, x, pl.ds(zl_ * 2, 2)], rx3.at[d - 1], at_z(d))

    def third_y(d):
        return late(
            1, 1, d, gy.at[e, zh, y, pl.ds(zl * 8 + ((x + d) % 4) * 2, 2)], ry3.at[d - 1], at_x(d)
        )

    def third_z(d):
        return late(
            1, 2, d, gz.at[e, zh, (y + d) % 4, zl, pl.ds(x * 2, 2)], rz3.at[d - 1], at_y(d)
        )

    for d in (1, 3, 2):
        second_x(d).start()

    for u in range(4):
        for d in (1, 2, 3):
            first_z(u + (4 if d == 2 else 0), d).wait_recv()

    @pl.loop(0, 4)
    def add_z1(v):
        acc = gz[e, zh, v, zl].astype(F32)
        for d in range(3):
            acc = acc + rz1[d, v].astype(F32)
        gz[e, zh, v, zl] = acc.astype(BF16)

    for d in (1, 3, 2):
        second_z(d).start()

    for it in range(8):
        for d in (1, 2, 3):
            first_y(it, d).wait_recv()

    @pl.loop(0, 8)
    def add_y1(s):
        h, k = s // 4, pl.ds((s % 4) * 4, 4)
        acc = gy[e, h, y, k].astype(F32)
        for d in range(3):
            acc = acc + ry1[d, h, k].astype(F32)
        gy[e, h, y, k] = acc.astype(BF16)

    for d in (1, 3, 2):
        second_y(d).start()

    for d in (1, 3, 2):
        second_x(d).wait_recv()
    for h in range(2):
        acc = gx[e, h, y, x].astype(F32)
        for d in range(3):
            acc = acc + rx2[d, h].astype(F32)
        gx[e, h, y, x] = acc.astype(BF16)
    for d in (1, 3, 2):
        third_x(d).start()

    for d in (1, 3, 2):
        second_z(d).wait_recv()
    k = pl.ds(x * 2, 2)
    for v in range(4):
        acc = gz[e, zh, v, zl, k].astype(F32)
        for d in range(3):
            acc = acc + rz2[d, v].astype(F32)
        gz[e, zh, v, zl, k] = acc.astype(BF16)
    for d in (1, 3, 2):
        third_z(d).start()

    for d in (1, 3, 2):
        second_y(d).wait_recv()
    k = pl.ds(zl * 8, 8)
    acc = gy[e, zh, y, k].astype(F32)
    for d in range(3):
        acc = acc + ry2[d].astype(F32)
    gy[e, zh, y, k] = acc.astype(BF16)
    for d in (1, 3, 2):
        third_y(d).start()

    for third in (third_x, third_z, third_y):
        for d in (1, 2, 3):
            third(d).wait_recv()
    acc_x = gx[e, zh, y, x, pl.ds(zl * 2, 2)].astype(F32)
    acc_y = gy[e, zh, y, pl.ds(zl * 8 + x * 2, 2)].astype(F32)
    acc_z = gz[e, zh, y, zl, pl.ds(x * 2, 2)].astype(F32)
    for d in range(3):
        acc_x = acc_x + rx3[d].astype(F32)
        acc_y = acc_y + ry3[d].astype(F32)
        acc_z = acc_z + rz3[d].astype(F32)
    for k in range(2):
        sums_out[:, k * 1024 : k * 1024 + WX] = acc_x[k]
        sums_out[:, k * 1024 + WX : k * 1024 + WX + WY] = acc_y[k]
        sums_out[:, k * 1024 + WX + WY : (k + 1) * 1024] = acc_z[k]

    for it in range(8):
        for copy in trade(it):
            copy.wait_send()
        if it % 4 != 3:
            first_x(it).wait_send()
        for d in (1, 2, 3):
            first_y(it, d).wait_send()
        for d in (1, 3) if it < 4 else (2,):
            first_z(it, d).wait_send()
    for copy in (second_x, second_y, second_z, third_x, third_y, third_z):
        for d in (1, 2, 3):
            copy(d).wait_send()


def on_device(spectra, offsets, groups, ctf, noise_weight, references):
    vmem = pl.BlockSpec(memory_space=pltpu.VMEM)
    anywhere = pl.BlockSpec(memory_space=pl.ANY)
    sem = pltpu.SemaphoreType.DMA
    sums, prob = pl.pallas_call(
        kernel,
        out_shape=(
            jax.ShapeDtypeStruct((16, 2048), F32),
            jax.ShapeDtypeStruct((1, IMG), F32),
        ),
        in_specs=[anywhere, anywhere] + [vmem] * 6,
        out_specs=(vmem, vmem),
        scratch_shapes=[
            pltpu.VMEM((2, 2, 4, 4, 4, 16, WX), BF16),
            pltpu.VMEM((2, 2, 4, 17, 16, WY), BF16),
            pltpu.VMEM((2, 2, 4, 2, 8, 16, WZ), BF16),
            pltpu.VMEM((2, 4, 4, 4, 16, WX), BF16),
            pltpu.VMEM((2, 4, 16, 16, WY), BF16),
            pltpu.VMEM((2, 4, 2, 8, 16, WZ), BF16),
            pltpu.VMEM((32, 512, IMG), BF16),
            pltpu.VMEM((16384, 128), F32),
            pltpu.VMEM((16, 2, 256, IMG), BF16),
            pltpu.VMEM((512, 128), F32),
            pltpu.VMEM((2, IMG, 16, 2 * A), BF16),
            pltpu.VMEM((2, 16, DEPTH, 2 * A), BF16),
            pltpu.VMEM((IMG, DEPTH), BF16),
            pltpu.VMEM((R, IMG), F32),
            pltpu.VMEM((3, 2, 2, 4, 2, 16, WX), BF16),
            pltpu.VMEM((3, 2, 16, 16, WY), BF16),
            pltpu.VMEM((3, 4, 8, 16, WZ), BF16),
            pltpu.VMEM((3, 2, 4, 16, WX), BF16),
            pltpu.VMEM((3, 8, 16, WY), BF16),
            pltpu.VMEM((3, 4, 2, 16, WZ), BF16),
            pltpu.VMEM((3, 2, 16, WX), BF16),
            pltpu.VMEM((3, 2, 16, WY), BF16),
            pltpu.VMEM((3, 2, 16, WZ), BF16),
            sem((4,)),
            sem((32,)),
            sem((32,)),
            sem((3, 8)),
            sem((3, 8)),
            sem((3, 2)),
            sem((3, 2)),
            sem((3, 8)),
            sem((3, 8)),
            sem((3, 4)),
            sem((3, 4)),
            sem((2, 3, 3)),
            sem((2, 3, 3)),
        ],
        compiler_params=pltpu.CompilerParams(
            collective_id=0, has_side_effects=True, vmem_limit_bytes=60 << 20
        ),
        cost_estimate=pl.CostEstimate(
            flops=14 << 30, bytes_accessed=24 << 20, transcendentals=1 << 20
        ),
        name="classify",
    )(
        spectra,
        jnp.asarray(shift_table()),
        offsets,
        groups.reshape(1, -1),
        ctf,
        noise_weight.reshape(1, -1),
        references,
        jnp.asarray(harmonic_rows()),
    )
    return sums, prob.reshape(-1)


def solution(mesh):
    placed = (
        P(("img", "cls"), None, None),
        P(("img", "cls"), None),
        P(("img", "cls")),
        P(),
        P(),
        P("cls", None),
    )
    return jax.shard_map(
        on_device,
        mesh=mesh,
        in_specs=placed,
        out_specs=(P("cls", "img"), P(("img", "cls"))),
        check_vma=False,
    )
```

time: 854 us -> 105 us (0.12)
  waiting for transfers between devices: 292 us -> 0 us
  matrix products: 235 us -> 0 us
  local copies, waits for them, and re-layouts: 153 us -> 4.27 us
  other arithmetic: 147 us -> 0 us
  Pallas kernels: 0 us -> 99.4 us
  between operations: 14.5 us -> 0.64 us
    ppermute x30 -> x0, waiting for transfers between devices: 254 us -> none  [shifted(): lax.ppermute(x, axis, [(i, (i + by) % devices) for i in range(devices)])]
    dot_general x67 -> x0, matrix products: 235 us -> none  [the longest x16 96.2 us: block_sums(): jnp.einsum('ncwj,njhk->cjwhk', wblock, stacked, preferred_element_type=jn...]
    pallas_call x0 -> x1, Pallas kernels: none -> 99.4 us  [on_device(): pl.pallas_call(kernel, out_shape=(jax.ShapeDtypeStruct((16, 2048), F32),...]
    mul x48 -> x0, local copies, waits for them, and re-layouts: 77.5 us -> none  [the longest x16 74.2 us: block_scores(): energy = jnp.sum(raw * raw, axis=(1, 2, 4))]
    reduce_sum x17 -> x0, other arithmetic: 67.9 us -> none  [the longest x16 65.1 us: block_scores(): energy = jnp.sum(raw * raw, axis=(1, 2, 4))]
    reduce_scatter x1 -> x0, waiting for transfers between devices: 37.2 us -> none  [on_device(): lax.psum_scatter(partial_sums.astype(jnp.bfloat16), 'img', scatter_dimens...]
    mul x35 -> x0, other arithmetic: 36.4 us -> none  [the longest x1 35.1 us: prepare(): shifted_re = contrast[:, :, None] * (real_part * cosine - imag_part * sine)]
    convert_element_type x19 -> x0, other arithmetic: 25.3 us -> none  [the longest x1 14 us: prepare(): values = spectra.astype(jnp.float32)]
  transfers between devices with their start and end apart: 31 -> 0, of which waited for: 31 -> 0; matrix products, arithmetic and copies ran while one was open for 13% -> 0% of each run, Pallas kernels for 0% -> 0%
where the time goes in v1:
time: 105 us; the launch traced here: 104 us
  Pallas kernels  99.4 us (95%)
  local copies, waits for them, and re-layouts  4.27 us (4%)
    pallas_call x1, Pallas kernels, on_device(): pl.pallas_call(kernel, out_shape=(jax.ShapeDtypeStruct((16, 2048), F32),...  99.4 us
    unnamed x3, local copies, waits for them, and re-layouts  4.27 us

profile of v1, /device:TPU:0, one launch (start us, length us, event | category | flops | bytes accessed | tf_op | source)
XLA Modules:
  0.0 104.3 jit_solution(2397027418904217186)
XLA Ops:
  0.6 1.5 %copy.10.offsets = s32[256,2]{1,0:T(8,128)} copy(s32[256,2]{0,1:T(2,128)} %param.9) | data formatting | bytes 4096 | tf_op args[1]
  2.1 99.4 %classify.1 = (f32[16,2048]{1,0:T(8,128)}, f32[1,256]{1,0:T(1,128)}) custom-call(bf16[256,64,256]{2,1,0:T(8,128)(2,1)} %spectra.1, bf16[64,384,256]{2,1,0:T(8,128)(2,1)} %constant.4.clone.table, s32[256,2]{1,0:T(8,128)} %copy.10.offsets, s32[1,256]{1,0:T(1,128)} %bitcast.4, f32[32,64]{1,0:T(8,128)} %ctf.1, f32[1,64]{1,0:T(1,128)} %bitcast.5, ...), custom_call_target="tpu_custom_call" | custom-call | flops 15032385536 | bytes 25165824 | tf_op jit(solution)/shard_map/classify/pallas_call | solution.py:621
  101.5 1.6 %copy.13 = f32[16,2048]{1,0:T(8,128)} copy(f32[16,2048]{1,0:T(8,128)} %get-tuple-element.8) | data formatting | bytes 262144
  103.1 1.2 %copy.14 = f32[256]{0:T(256)} copy(f32[256]{0:T(256)} %bitcast.3) | data formatting | bytes 2048

commit v2 on v1

v2 whole, which is shorter than its diff:
```python
import math

import jax
import jax.numpy as jnp
import ml_dtypes
import numpy as np
from jax import lax
from jax.experimental import pallas as pl
from jax.experimental.pallas import tpu as pltpu
from jax.sharding import PartitionSpec as P

MESH = pl.DeviceIdType.MESH
F32 = jnp.float32
BF16 = jnp.bfloat16
HIGHEST = lax.Precision.HIGHEST

IMG = 256
R = 64
A = 128
ROTS = 16
SHIFTS = 13
KINDS = (SHIFTS * SHIFTS + 1) // 2
LOW = 88
DEPTH = 176
WX, WY, WZ = 384, 256, 384

S1 = math.sqrt(0.5)
C1 = math.cos(math.pi / 8)
C3 = math.cos(3 * math.pi / 8)


def split_np(values):
    high = values.astype(np.float32).astype(ml_dtypes.bfloat16)
    low = (values - high.astype(np.float64)).astype(np.float32).astype(ml_dtypes.bfloat16)
    return high, low


def shift_table():
    theta = 2.0 * np.pi * np.arange(A) / A
    radius = np.arange(R) + 1.0
    step = np.arange(SHIFTS) - 6.0
    along = (
        np.cos(theta)[None, None, :] * step[:, None, None]
        + np.sin(theta)[None, None, :] * step[None, :, None]
    ).reshape(SHIFTS * SHIFTS, A)[:KINDS]
    phase = -2.0 * np.pi * radius[:, None, None] * along[None] / (2.0 * R)
    both = np.concatenate([np.cos(phase), np.sin(phase)], axis=-1)
    high, low = split_np(both)
    table = np.zeros((R, DEPTH, 2 * A), ml_dtypes.bfloat16)
    table[:, :KINDS] = high
    table[:, LOW : LOW + KINDS] = low
    return table


def harmonic_rows():
    quarter = A // ROTS
    orders = ROTS * np.arange(quarter)[None, :] + np.arange(ROTS)[:, None]
    turns = (np.arange(A)[:, None, None] * orders[None]) % A
    angle = 2.0 * np.pi * turns / A
    upper = np.stack([np.cos(angle), -np.sin(angle)], axis=2)
    lower = np.stack([np.sin(angle), np.cos(angle)], axis=2)
    table = np.concatenate([upper, lower], axis=0) / math.sqrt(A)
    return np.ascontiguousarray(table.reshape(2 * A, 2 * A).T).astype(np.float32).astype(
        ml_dtypes.bfloat16
    )


def cosine_part(a):
    p, m = a[0] + a[8], a[0] - a[8]
    t, d = a[2] + a[6], S1 * (a[2] - a[6])
    q = p + a[4]
    even = [q + t, m + d, p - a[4], m - d, q - t]
    s17, d17 = a[1] + a[7], a[1] - a[7]
    s35, d35 = a[3] + a[5], a[3] - a[5]
    odd = [s17 + s35, C1 * d17 + C3 * d35, S1 * (s17 - s35), C3 * d17 - C1 * d35]
    out = [even[k] + odd[k] for k in range(4)] + [even[4]]
    return out + [even[k] - odd[k] for k in (3, 2, 1, 0)]


def sine_part(b):
    t = S1 * (b[2] + b[6])
    even = [None, t + b[4], b[2] - b[6], t - b[4]]
    s17, d17 = b[1] + b[7], b[1] - b[7]
    s35, d35 = b[3] + b[5], b[3] - b[5]
    odd = [None, C3 * s17 + C1 * s35, S1 * (d17 + d35), C1 * s17 - C3 * s35, d17 - d35]
    out = [None] + [odd[k] + even[k] for k in (1, 2, 3)] + [odd[4]]
    return out + [odd[k] - even[k] for k in (3, 2, 1)]


def across(a, b, precision=None):
    return lax.dot_general(
        a, b, (((1,), (1,)), ((), ())), precision=precision, preferred_element_type=F32
    )


def plain(a, b, precision=None):
    return jnp.dot(a, b, precision=precision, preferred_element_type=F32)


def kernel(
    spectra, table, offsets, groups, ctf, noise, refs, harmonics,
    sums_out, prob_out,
    gx, gy, gz, gt, cx, cy, cz, ht, qb, wb, norm, spec, tab, moved, hot, sign, cgt,
    rx1, ry1, rz1, rx2, ry2, rz2, rx3, ry3, rz3,
    dma, ag_s, ag_r, core_s, core_r, x1_s, x1_r, y1_s, y1_r, z1_s, z1_r, late_s, late_r,
):
    img = lax.axis_index("img")
    cls = lax.axis_index("cls")
    zl, x = img // 4, img % 4
    zh, y, e = cls // 8, (cls // 2) % 4, cls % 2
    other = 1 - e

    def device(zl_, x_, zh_, y_, e_):
        return (zl_ * 4 + x_, zh_ * 8 + y_ * 2 + e_)

    def at_x(d):
        return device(zl, (x + d) % 4, zh, y, e)

    def at_y(d):
        return device(zl, x, zh, (y + d) % 4, e)

    def flip(d):
        return (zh + d // 2) % 2, (zl + d) % 2

    def at_z(d):
        zh_, zl_ = flip(d)
        return device(zl_, x, zh_, y, e)

    def at_zy(d):
        return device((zl + 1) % 2, x, (zh + 1) % 2, (y + d) % 4, e)

    twin = device(zl, x, zh, y, other)

    def remote(src, dst, send, recv, where):
        return pltpu.make_async_remote_copy(
            src_ref=src, dst_ref=dst, send_sem=send, recv_sem=recv,
            device_id=where, device_id_type=MESH,
        )

    def spec_copy(c):
        return pltpu.make_async_copy(
            spectra.at[:, pl.ds(c * 16, 16), :], spec.at[c % 2], dma.at[c % 2]
        )

    def tab_copy(c):
        return pltpu.make_async_copy(
            table.at[pl.ds(c * 16, 16)], tab.at[c % 2], dma.at[2 + c % 2]
        )

    barrier = pltpu.get_barrier_semaphore()
    friends = [twin]
    friends += [at_x(d) for d in (1, 2, 3)]
    friends += [at_y(d) for d in (1, 2, 3)]
    friends += [at_z(d) for d in (1, 2, 3)]
    friends += [at_zy(d) for d in (1, 2, 3)]
    for friend in friends:
        pl.semaphore_signal(barrier, inc=1, device_id=friend, device_id_type=MESH)
    spec_copy(0).start()
    tab_copy(0).start()

    spread = (
        lax.broadcasted_iota(jnp.int32, (R, 512), 0)
        == lax.broadcasted_iota(jnp.int32, (R, 512), 1) // 8
    ).astype(F32)
    nw = jnp.broadcast_to(noise[...], (8, R))
    nwx = plain(nw, spread, HIGHEST)[0:1]

    def weighted(j, first, width, gains):
        start = j * 1024 + first
        part = refs[:, pl.ds(pl.multiple_of(start, 128), width)].astype(F32)
        return (part * gains).astype(BF16)

    gain_x = nwx[:, :384]
    gain_y = jnp.concatenate([nwx[:, 384:], nwx[:, :128]], axis=1)
    gain_z = nwx[:, 128:]
    for h in range(2):
        for k in range(2):
            gx[e, zh, y, x, h, k] = weighted(k * 8 + x * 2 + h, 0, WX, gain_x)
        for k in range(4):
            gz[e, zh, y, zl, h, k] = weighted(zl * 8 + k * 2 + h, WX + WY, WZ, gain_z)
        for k in range(8):
            gy[e, zh, y, h, k // 2, k % 2] = weighted(
                (k % 2) * 8 + (k // 2) * 2 + h, WX, WY, gain_y
            )

    def ag(h, index, piece, where):
        return remote(piece, piece, ag_s.at[h, index], ag_r.at[h, index], where)

    def pre_x(h):
        mine = gx.at[e, zh, y, x, h]
        out = [ag(h, d - 1, mine, at_y(d)) for d in (1, 3, 2)] + [ag(h, 3, mine, at_z(3))]
        return out + [ag(h, 3 + d, mine, at_zy(d)) for d in (1, 3, 2)]

    def pre_z(h):
        return [ag(h, 6 + d, gz.at[e, zh, y, zl, h], at_y(d)) for d in (1, 3, 2)]

    def pre_y(h):
        return [ag(h, 10, gy.at[e, zh, y, h], at_z(3))]

    pre_t = ag(0, 32, gt.at[e, zh, y], at_z(3))

    def piece_x(h, e_, d):
        return gx.at[e_, :, :, (x + d) % 4, h]

    def piece_y(h, e_, d):
        return gy.at[e_, :, (y + d) % 4, h]

    def piece_z(h, e_, d):
        zh_, zl_ = flip(d)
        return gz.at[e_, zh_, :, zl_, h]

    def last_x(h, d):
        return ag(h, 10 + d, piece_x(h, e, 0), at_x(d))

    def last_y(h, d):
        return ag(h, 13 + d, piece_y(h, e, 0), at_y(d))

    def last_z(h, d):
        return ag(h, 16 + d, piece_z(h, e, 0), at_z(d))

    def last_t(d):
        return ag(0, 32 + d, gt.at[e, :, y], at_y(d))

    pieces = (piece_x, piece_y, piece_z)
    lasts = (last_x, last_y, last_z)

    def share(h, group, d):
        return ag(h, 20 + 4 * group + d, pieces[group](h, e, d), twin)

    def share_t(d):
        return ag(0, 36 + d, gt.at[e, :, (y + d) % 4], twin)

    pl.semaphore_wait(barrier, len(friends))
    for h in range(2):
        for copy in pre_x(h) + pre_z(h) + pre_y(h):
            copy.start()

    total = jnp.zeros((16, 512), F32)
    for k in range(32):
        part = refs[:, k * 512 : (k + 1) * 512].astype(F32)
        total = total + part * part
    ctf4 = jnp.concatenate([ctf[...]] * 4, axis=0)
    by_group = plain(0.5 * noise[...] * ctf4 * ctf4, spread, HIGHEST)
    energy = across(total, by_group, HIGHEST)
    high = energy.astype(BF16).astype(F32)
    middle = (energy - high).astype(BF16).astype(F32)
    low = energy - high - middle
    lane = lax.broadcasted_iota(jnp.int32, (16, 128), 1) // 32
    gt[e, zh, y] = jnp.where(
        lane == 0, high, jnp.where(lane == 1, middle, jnp.where(lane == 2, low, 0.0))
    ).astype(BF16)
    pre_t.start()

    index = (offsets[0:1, :] + 6) * SHIFTS + offsets[1:2, :] + 6
    index = jnp.transpose(jnp.broadcast_to(index.astype(F32), (128, IMG)))
    upper = SHIFTS * SHIFTS - 1.0
    sign[...] = jnp.where(index < KINDS, 1.0, -1.0)
    kind = jnp.minimum(index, upper - index)[:, 0:1]
    column = lax.broadcasted_iota(jnp.int32, (IMG, DEPTH), 1).astype(F32)
    hot[...] = ((column == kind) | (column == kind + LOW)).astype(F32).astype(BF16)
    of_group = (
        lax.broadcasted_iota(jnp.int32, (32, IMG), 0) == groups[...]
    ).astype(F32)
    cgt[...] = lax.dot_general(
        ctf[...], of_group, (((0,), (0,)), ((), ())), precision=HIGHEST, preferred_element_type=F32
    )

    def prepare(c):
        slot = c % 2
        if c < 3:
            spec_copy(c + 1).start()
            tab_copy(c + 1).start()
        spec_copy(c).wait()
        tab_copy(c).wait()

        @pl.loop(0, 16)
        def widen(b):
            part = spec[slot, pl.ds(b * 16, 16)].astype(F32)
            rows = pl.ds(pl.multiple_of(b * 256, 256), 256)
            qb[rows, :] = part[:, :, :A].reshape(256, A)
            rows = pl.ds(pl.multiple_of(4096 + b * 256, 256), 256)
            qb[rows, :] = part[:, :, A:].reshape(256, A)

        @pl.loop(0, 2)
        def move(b):
            for k in range(8):
                r = b * 8 + k
                turn = plain(hot[...], tab[slot, r])
                cosine, sine = turn[:, :A], turn[:, A:] * sign[...]
                real = qb[pl.ds(r, IMG, stride=16), :]
                imag = qb[pl.ds(4096 + r, IMG, stride=16), :]
                moved[r] = jnp.concatenate(
                    [real * cosine - imag * sine, real * sine + imag * cosine], axis=1
                ).astype(BF16)

        @pl.loop(0, 2)
        def transform(b):
            found = []
            for k in range(8):
                r = b * 8 + k
                out = across(harmonics[...], moved[r]) * cgt[pl.ds(c * 16 + r, 1), :]
                found.append(out.reshape(32, 8, IMG))
            both = jnp.concatenate(found, axis=1)
            ht[:, pl.ds(pl.multiple_of(c * 128 + b * 64, 64), 64), :] = both.astype(BF16)

    def pass_on(h):
        for copy in pre_x(h):
            copy.wait_recv()
        for d in (1, 3, 2):
            last_x(h, d).start()
        for copy in pre_z(h) + pre_y(h):
            copy.wait_recv()
        for d in (1, 3, 2):
            last_z(h, d).start()
            last_y(h, d).start()
        if h == 0:
            pre_t.wait_recv()
            for d in (1, 3, 2):
                last_t(d).start()
            share_t(0).start()
        for group in range(3):
            share(h, group, 0).start()

    def hand_over(h):
        for d in (1, 3, 2):
            for group in (1, 0, 2):
                lasts[group](h, d).wait_recv()
                share(h, group, d if group == 2 else 4 - d).start()
            if h == 0:
                last_t(d).wait_recv()
                share_t(4 - d).start()
        for d in range(4):
            for group in range(3):
                share(h, group, d).wait_recv()
            if h == 0:
                share_t(d).wait_recv()

    def correlate(h):
        @pl.loop(0, 4)
        def _(k):
            for zv in range(2):
                j = zv * 8 + k * 2 + h
                part_x = gx[:, :, :, k, h, zv].reshape(256, WX)
                part_y = gy[:, :, :, h, k, zv].reshape(256, WY)
                part_z = gz[:, :, :, zv, h, k].reshape(256, WZ)
                real = jnp.concatenate([part_x, part_y[:, :128]], axis=1)
                imag = jnp.concatenate([part_y[:, 128:], part_z], axis=1)
                h_re, h_im = ht[2 * j], ht[2 * j + 1]
                q_re = plain(real, h_re) + plain(imag, h_im)
                q_im = plain(imag, h_re) - plain(real, h_im)
                for t in range(2):
                    base = pl.multiple_of((t * 32 + 2 * j) * 256, 256)
                    qb[pl.ds(base, 256), :] = q_re[:, t * 128 : (t + 1) * 128]
                    qb[pl.ds(base + 256, 256), :] = q_im[:, t * 128 : (t + 1) * 128]

    prepare(0)
    pass_on(0)
    prepare(1)
    pass_on(1)
    prepare(2)
    prepare(3)
    hand_over(0)
    correlate(0)
    hand_over(1)
    correlate(1)

    row = lax.broadcasted_iota(jnp.int32, (128, IMG), 0)
    thrice = ((row % 32 == groups[...]) & (row < 96)).astype(F32).astype(BF16)
    norms = plain(gt[...].reshape(256, 128), thrice)
    norm[0:256, :] = norms[:, :128]
    norm[256:512, :] = norms[:, 128:]

    for t in range(2):
        def at(k, c, t=t):
            return (t * 32 + k) * 256 + c

        def scores(b, top, t=t, at=at):
            c = pl.multiple_of(b * 8, 8)
            re = [qb[pl.ds(at(2 * j, c), 8), :] for j in range(16)]
            im = [qb[pl.ds(at(2 * j + 1, c), 8), :] for j in range(16)]
            a = [re[0]] + [re[j] + re[16 - j] for j in range(1, 8)] + [re[8]]
            s = [None] + [im[j] - im[16 - j] for j in range(1, 8)]
            a[0] = a[0] - norm[pl.ds(t * 256 + c, 8), :]
            cp, sp = cosine_part(a), sine_part(s)
            out = [cp[0]] + [cp[k] + sp[k] for k in range(1, 8)] + [cp[8]]
            out += [cp[16 - k] - sp[16 - k] for k in range(9, 16)]
            for k in range(16):
                qb[pl.ds(at(k, c), 8), :] = out[k]
                top = jnp.maximum(top, out[k])
            return top

        top = lax.fori_loop(0, 32, scores, jnp.full((8, 128), -jnp.inf, F32))
        top = jnp.max(top, axis=0, keepdims=True)

        def exponents(b, total, top=top, at=at):
            c = pl.multiple_of(b * 8, 8)
            for k in range(16):
                value = jnp.exp(qb[pl.ds(at(k, c), 8), :] - top)
                qb[pl.ds(at(k, c), 8), :] = value
                total = total + value
            return total

        total = lax.fori_loop(0, 32, exponents, jnp.zeros((8, 128), F32))
        scale = 1.0 / jnp.sum(total, axis=0, keepdims=True)
        prob_out[:, t * 128 : (t + 1) * 128] = scale

        @pl.loop(0, 16)
        def back(b, t=t, at=at, scale=scale):
            c = pl.multiple_of(b * 16, 16)
            p = [qb[pl.ds(at(k, c), 16), :] * scale for k in range(16)]
            a = [p[0]] + [p[k] + p[16 - k] for k in range(1, 8)] + [p[8]]
            s = [None] + [p[k] - p[16 - k] for k in range(1, 8)]
            cp, sp = cosine_part(a), sine_part(s)
            cols = slice(t * 128, (t + 1) * 128)
            zero = jnp.zeros((16, 128), BF16)
            for j in range(9):
                re = cp[j].astype(BF16)
                wb[j, 0, pl.ds(c, 16), cols] = re
                if j in (0, 8):
                    wb[j, 1, pl.ds(c, 16), cols] = zero
                else:
                    wb[16 - j, 0, pl.ds(c, 16), cols] = re
                    wb[j, 1, pl.ds(c, 16), cols] = sp[j].astype(BF16)
                    wb[16 - j, 1, pl.ds(c, 16), cols] = (-sp[j]).astype(BF16)

    for h in range(2):
        for copy in pre_x(h) + pre_y(h) + pre_z(h):
            copy.wait_send()
        for group in range(3):
            for d in (1, 2, 3):
                lasts[group](h, d).wait_send()
            for d in range(4):
                share(h, group, d).wait_send()
    pre_t.wait_send()
    for d in (1, 2, 3):
        last_t(d).wait_send()
    for d in range(4):
        share_t(d).wait_send()

    def target(it):
        return (x + 1 + it) % 4, it // 4

    def trade(it):
        xt, h = target(it)
        pairs = (
            (gx.at[other, :, :, xt, h], cx.at[:, :, xt, h]),
            (gy.at[other, :, :, h, xt], cy.at[:, :, h, xt]),
            (gz.at[other, :, :, :, h, xt], cz.at[:, :, :, h, xt]),
        )
        return [
            remote(src, dst, core_s.at[k, it], core_r.at[k, it], twin)
            for k, (src, dst) in enumerate(pairs)
        ]

    def first_x(it):
        xt, h = target(it)
        u = it % 4
        return remote(
            gx.at[e, :, :, xt, h], rx1.at[u, h], x1_s.at[u, h], x1_r.at[u, h], at_x(u + 1)
        )

    def first_y(it, d):
        xt, h = target(it)
        return remote(
            gy.at[e, :, (y + d) % 4, h, xt], ry1.at[d - 1, h, :, xt],
            y1_s.at[d - 1, it], y1_r.at[d - 1, it], at_y(d),
        )

    def first_z(it, d):
        xt, h = target(it)
        zh_, zl_ = flip(d)
        return remote(
            gz.at[e, zh_, :, zl_, h, xt], rz1.at[d - 1, h, :, xt],
            z1_s.at[d - 1, it], z1_r.at[d - 1, it], at_z(d),
        )

    def settle(it):
        xt, h = target(it)
        for copy in trade(it):
            copy.wait_recv()

        @pl.loop(0, 8)
        def add(s):
            w, v = s // 4, s % 4
            gx[e, w, v, xt, h] = (
                gx[e, w, v, xt, h].astype(F32) + cx[w, v, xt, h].astype(F32)
            ).astype(BF16)
            gy[e, w, v, h, xt] = (
                gy[e, w, v, h, xt].astype(F32) + cy[w, v, h, xt].astype(F32)
            ).astype(BF16)
            gz[e, w, v, :, h, xt] = (
                gz[e, w, v, :, h, xt].astype(F32) + cz[w, v, :, h, xt].astype(F32)
            ).astype(BF16)

        @pl.when(it % 4 != 3)
        def _():
            first_x(it).start()

        for d in (1, 3, 2):
            first_z(it, d).start()
            first_y(it, d).start()

    @pl.loop(0, 8)
    def accumulate(it):
        xt, h = target(it)
        for zv in range(2):
            j = zv * 8 + xt * 2 + h
            w_re, w_im = wb[j, 0], wb[j, 1]
            w_minus = wb[(16 - j) % 16, 1]
            h_both = jnp.concatenate([ht[2 * j], ht[2 * j + 1]], axis=1)
            out_re = across(jnp.concatenate([w_re, w_minus], axis=1), h_both).astype(BF16)
            out_im = across(jnp.concatenate([w_im, w_re], axis=1), h_both).astype(BF16)
            gx[:, :, :, xt, h, zv] = out_re[:, :384].reshape(2, 2, 4, 16, WX)
            gy[:, :, :, h, xt, zv] = jnp.concatenate(
                [out_re[:, 384:], out_im[:, :128]], axis=1
            ).reshape(2, 2, 4, 16, WY)
            gz[:, :, :, zv, h, xt] = out_im[:, 128:].reshape(2, 2, 4, 16, WZ)
        for copy in trade(it):
            copy.start()

        @pl.when(it > 0)
        def _():
            settle(it - 1)

    settle(7)

    def late(stage, group, h, d, src, dst, where):
        return remote(
            src, dst.at[d - 1, h], late_s.at[stage, group, h, d - 1],
            late_r.at[stage, group, h, d - 1], where,
        )

    def second_x(h, d):
        return late(0, 0, h, d, gx.at[e, :, (y + d) % 4, x, h], rx2, at_y(d))

    def second_y(h, d):
        zh_, zl_ = flip(d)
        return late(0, 1, h, d, gy.at[e, zh_, y, h, :, zl_], ry2, at_z(d))

    def second_z(h, d):
        return late(0, 2, h, d, gz.at[e, zh, :, zl, h, (x + d) % 4], rz2, at_x(d))

    def third_x(h, d):
        zh_, zl_ = flip(d)
        return late(1, 0, h, d, gx.at[e, zh_, y, x, h, zl_], rx3, at_z(d))

    def third_y(h, d):
        return late(1, 1, h, d, gy.at[e, zh, y, h, (x + d) % 4, zl], ry3, at_x(d))

    def third_z(h, d):
        return late(1, 2, h, d, gz.at[e, zh, (y + d) % 4, zl, h, x], rz3, at_y(d))

    def total_of(own, parts):
        acc = own.astype(F32)
        for part in parts:
            acc = acc + part.astype(F32)
        return acc

    for h in range(2):
        for u in range(3):
            first_x(u + 4 * h).wait_recv()

        @pl.loop(0, 8)
        def add_x1(s, h=h):
            w, v = s // 4, s % 4
            gx[e, w, v, x, h] = total_of(
                gx[e, w, v, x, h], [rx1[u, h, w, v] for u in range(3)]
            ).astype(BF16)

        for d in (1, 3, 2):
            second_x(h, d).start()
        for it in range(4 * h, 4 * h + 4):
            for d in (1, 2, 3):
                first_z(it, d).wait_recv()

        @pl.loop(0, 4)
        def add_z1(v, h=h):
            gz[e, zh, v, zl, h] = total_of(
                gz[e, zh, v, zl, h], [rz1[d, h, v] for d in range(3)]
            ).astype(BF16)

        for d in (1, 3, 2):
            second_z(h, d).start()
        for it in range(4 * h, 4 * h + 4):
            for d in (1, 2, 3):
                first_y(it, d).wait_recv()

        @pl.loop(0, 8)
        def add_y1(s, h=h):
            w, k = s // 4, s % 4
            gy[e, w, y, h, k] = total_of(
                gy[e, w, y, h, k], [ry1[d, h, w, k] for d in range(3)]
            ).astype(BF16)

        for d in (1, 3, 2):
            second_y(h, d).start()

    for h in range(2):
        for d in (1, 3, 2):
            second_x(h, d).wait_recv()
        gx[e, :, y, x, h] = total_of(
            gx[e, :, y, x, h], [rx2[d, h] for d in range(3)]
        ).astype(BF16)
        for d in (1, 3, 2):
            third_x(h, d).start()
        for d in (1, 3, 2):
            second_z(h, d).wait_recv()
        gz[e, zh, :, zl, h, x] = total_of(
            gz[e, zh, :, zl, h, x], [rz2[d, h] for d in range(3)]
        ).astype(BF16)
        for d in (1, 3, 2):
            third_z(h, d).start()
        for d in (1, 3, 2):
            second_y(h, d).wait_recv()
        gy[e, zh, y, h, :, zl] = total_of(
            gy[e, zh, y, h, :, zl], [ry2[d, h] for d in range(3)]
        ).astype(BF16)
        for d in (1, 3, 2):
            third_y(h, d).start()

    for h in range(2):
        first = h * 1024
        for third in (third_x, third_z, third_y):
            for d in (1, 2, 3):
                third(h, d).wait_recv()
        sums_out[:, first : first + WX] = total_of(
            gx[e, zh, y, x, h, zl], [rx3[d, h] for d in range(3)]
        )
        sums_out[:, first + WX : first + WX + WY] = total_of(
            gy[e, zh, y, h, x, zl], [ry3[d, h] for d in range(3)]
        )
        sums_out[:, first + WX + WY : first + 1024] = total_of(
            gz[e, zh, y, zl, h, x], [rz3[d, h] for d in range(3)]
        )

    for it in range(8):
        for copy in trade(it):
            copy.wait_send()
        if it % 4 != 3:
            first_x(it).wait_send()
        for d in (1, 2, 3):
            first_y(it, d).wait_send()
            first_z(it, d).wait_send()
    for copy in (second_x, second_y, second_z, third_x, third_y, third_z):
        for h in range(2):
            for d in (1, 2, 3):
                copy(h, d).wait_send()


def on_device(spectra, offsets, groups, ctf, noise_weight, references):
    vmem = pl.BlockSpec(memory_space=pltpu.VMEM)
    anywhere = pl.BlockSpec(memory_space=pl.ANY)
    sem = pltpu.SemaphoreType.DMA
    sums, prob = pl.pallas_call(
        kernel,
        out_shape=(
            jax.ShapeDtypeStruct((16, 2048), F32),
            jax.ShapeDtypeStruct((1, IMG), F32),
        ),
        in_specs=[anywhere, anywhere] + [vmem] * 6,
        out_specs=(vmem, vmem),
        scratch_shapes=[
            pltpu.VMEM((2, 2, 4, 4, 2, 2, 16, WX), BF16),
            pltpu.VMEM((2, 2, 4, 2, 4, 2, 16, WY), BF16),
            pltpu.VMEM((2, 2, 4, 2, 2, 4, 16, WZ), BF16),
            pltpu.VMEM((2, 2, 4, 16, 128), BF16),
            pltpu.VMEM((2, 4, 4, 2, 2, 16, WX), BF16),
            pltpu.VMEM((2, 4, 2, 4, 2, 16, WY), BF16),
            pltpu.VMEM((2, 4, 2, 2, 4, 16, WZ), BF16),
            pltpu.VMEM((32, 512, IMG), BF16),
            pltpu.VMEM((16384, 128), F32),
            pltpu.VMEM((16, 2, 256, IMG), BF16),
            pltpu.VMEM((512, 128), F32),
            pltpu.VMEM((2, IMG, 16, 2 * A), BF16),
            pltpu.VMEM((2, 16, DEPTH, 2 * A), BF16),
            pltpu.VMEM((16, IMG, 2 * A), BF16),
            pltpu.VMEM((IMG, DEPTH), BF16),
            pltpu.VMEM((IMG, A), F32),
            pltpu.VMEM((R, IMG), F32),
            pltpu.VMEM((3, 2, 2, 4, 2, 16, WX), BF16),
            pltpu.VMEM((3, 2, 2, 4, 2, 16, WY), BF16),
            pltpu.VMEM((3, 2, 4, 4, 16, WZ), BF16),
            pltpu.VMEM((3, 2, 2, 2, 16, WX), BF16),
            pltpu.VMEM((3, 2, 4, 16, WY), BF16),
            pltpu.VMEM((3, 2, 4, 16, WZ), BF16),
            pltpu.VMEM((3, 2, 16, WX), BF16),
            pltpu.VMEM((3, 2, 16, WY), BF16),
            pltpu.VMEM((3, 2, 16, WZ), BF16),
            sem((4,)),
            sem((2, 40)),
            sem((2, 40)),
            sem((3, 8)),
            sem((3, 8)),
            sem((3, 2)),
            sem((3, 2)),
            sem((3, 8)),
            sem((3, 8)),
            sem((3, 8)),
            sem((3, 8)),
            sem((2, 3, 2, 3)),
            sem((2, 3, 2, 3)),
        ],
        compiler_params=pltpu.CompilerParams(
            collective_id=0, has_side_effects=True, vmem_limit_bytes=60 << 20
        ),
        cost_estimate=pl.CostEstimate(
            flops=14 << 30, bytes_accessed=24 << 20, transcendentals=1 << 20
        ),
        name="classify",
    )(
        spectra,
        jnp.asarray(shift_table()),
        offsets.T,
        groups.reshape(1, -1),
        ctf,
        noise_weight.reshape(1, -1),
        references,
        jnp.asarray(harmonic_rows()),
    )
    return sums, prob.reshape(-1)


def solution(mesh):
    placed = (
        P(("img", "cls"), None, None),
        P(("img", "cls"), None),
        P(("img", "cls")),
        P(),
        P(),
        P("cls", None),
    )
    return jax.shard_map(
        on_device,
        mesh=mesh,
        in_specs=placed,
        out_specs=(P("cls", "img"), P(("img", "cls"))),
        check_vma=False,
    )
```

time: 105 us -> 85.7 us (0.82)
  Pallas kernels: 99.4 us -> 82.1 us
  local copies, waits for them, and re-layouts: 4.27 us -> 2.8 us
    pallas_call x1, Pallas kernels: 99.4 us -> 82.1 us  [on_device(): pl.pallas_call(kernel, out_shape=(jax.ShapeDtypeStruct((16, 2048), F32),...]
    unnamed x3 -> x2, local copies, waits for them, and re-layouts: 4.27 us -> 2.8 us
where the time goes in v2:
time: 85.7 us; the launch traced here: 85.6 us
  Pallas kernels  82.1 us (96%)
  local copies, waits for them, and re-layouts  2.8 us (3%)
    pallas_call x1, Pallas kernels, on_device(): pl.pallas_call(kernel, out_shape=(jax.ShapeDtypeStruct((16, 2048), F32),...  82.1 us
    unnamed x2, local copies, waits for them, and re-layouts  2.8 us

profile of v2, /device:TPU:0, one launch (start us, length us, event | category | flops | bytes accessed | tf_op | source)
XLA Modules:
  0.0 85.6 jit_solution(4123733097343239695)
XLA Ops:
  0.6 82.1 %classify.1 = (f32[16,2048]{1,0:T(8,128)}, f32[1,256]{1,0:T(1,128)}) custom-call(bf16[256,64,256]{2,1,0:T(8,128)(2,1)} %spectra.1, bf16[64,176,256]{2,1,0:T(8,128)(2,1)} %constant.4.clone.table, s32[2,256]{1,0:T(2,128)} %bitcast.5, s32[1,256]{1,0:T(1,128)} %bitcast.6, f32[32,64]{1,0:T(8,128)} %ctf.1, f32[1,64]{1,0:T(1,128)} %bitcast.7, ...), custom_call_target="tpu_custom_call" | custom-call | flops 15032385536 | bytes 25165824 | tf_op jit(solution)/shard_map/classify/pallas_call | solution.py:654
  82.8 1.6 %copy.12 = f32[16,2048]{1,0:T(8,128)} copy(f32[16,2048]{1,0:T(8,128)} %get-tuple-element.8) | data formatting | bytes 262144
  84.4 1.2 %copy.13 = f32[256]{0:T(256)} copy(f32[256]{0:T(256)} %bitcast.4) | data formatting | bytes 2048

commit v3 on v2

--- a/solution.py
+++ b/solution.py
@@ -23,6 +23,8 @@
 LOW = 88
 DEPTH = 176
 WX, WY, WZ = 384, 256, 384
+
+SETTLE, FINISH = 3, 6
 
 S1 = math.sqrt(0.5)
 C1 = math.cos(math.pi / 8)
@@ -101,8 +103,9 @@
     spectra, table, offsets, groups, ctf, noise, refs, harmonics,
     sums_out, prob_out,
     gx, gy, gz, gt, cx, cy, cz, ht, qb, wb, norm, spec, tab, moved, hot, sign, cgt,
-    rx1, ry1, rz1, rx2, ry2, rz2, rx3, ry3, rz3,
-    dma, ag_s, ag_r, core_s, core_r, x1_s, x1_r, y1_s, y1_r, z1_s, z1_r, late_s, late_r,
+    qx, qz, rx1, ry1, rz1, rx2, ry2, rz2, rx3, ry3, rz3,
+    dma, ag_s, ag_r, core_s, core_r, qx_s, qx_r, qz_s, qz_r,
+    x1_s, x1_r, y1_s, y1_r, z1_s, z1_r, late_s, late_r,
 ):
     img = lax.axis_index("img")
     cls = lax.axis_index("cls")
@@ -126,9 +129,6 @@
         zh_, zl_ = flip(d)
         return device(zl_, x, zh_, y, e)
 
-    def at_zy(d):
-        return device((zl + 1) % 2, x, (zh + 1) % 2, (y + d) % 4, e)
-
     twin = device(zl, x, zh, y, other)
 
     def remote(src, dst, send, recv, where):
@@ -152,7 +152,6 @@
     friends += [at_x(d) for d in (1, 2, 3)]
     friends += [at_y(d) for d in (1, 2, 3)]
     friends += [at_z(d) for d in (1, 2, 3)]
-    friends += [at_zy(d) for d in (1, 2, 3)]
     for friend in friends:
         pl.semaphore_signal(barrier, inc=1, device_id=friend, device_id_type=MESH)
     spec_copy(0).start()
@@ -186,10 +185,11 @@
     def ag(h, index, piece, where):
         return remote(piece, piece, ag_s.at[h, index], ag_r.at[h, index], where)
 
+    def flip_x(h):
+        return ag(h, 3, gx.at[e, zh, y, x, h], at_z(3))
+
     def pre_x(h):
-        mine = gx.at[e, zh, y, x, h]
-        out = [ag(h, d - 1, mine, at_y(d)) for d in (1, 3, 2)] + [ag(h, 3, mine, at_z(3))]
-        return out + [ag(h, 3 + d, mine, at_zy(d)) for d in (1, 3, 2)]
+        return [ag(h, d - 1, gx.at[e, :, y, x, h], at_y(d)) for d in (1, 3, 2)]
 
     def pre_z(h):
         return [ag(h, 6 + d, gz.at[e, zh, y, zl, h], at_y(d)) for d in (1, 3, 2)]
@@ -218,6 +218,17 @@
     def last_z(h, d):
         return ag(h, 16 + d, piece_z(h, e, 0), at_z(d))
 
+    def relays(h):
+        z_1, z_3 = flip(1), flip(3)
+        return [
+            ag(h, 4, gx.at[e, 0, :, (x + 3) % 4, h], at_x(1)),
+            ag(h, 5, gx.at[e, 1, :, (x + 1) % 4, h], at_x(3)),
+            ag(h, 6, gy.at[e, 0, (y + 3) % 4, h], at_y(1)),
+            ag(h, 12, gy.at[e, 1, (y + 1) % 4, h], at_y(3)),
+            ag(h, 15, gz.at[e, z_3[0], pl.ds(0, 2), z_3[1], h], at_z(1)),
+            ag(h, 18, gz.at[e, z_1[0], pl.ds(2, 2), z_1[1], h], at_z(3)),
+        ]
+
     def last_t(d):
         return ag(0, 32 + d, gt.at[e, :, y], at_y(d))
 
@@ -231,8 +242,13 @@
         return ag(0, 36 + d, gt.at[e, :, (y + d) % 4], twin)
 
     pl.semaphore_wait(barrier, len(friends))
+    flip_x(0).start()
+    flip_x(1).start()
     for h in range(2):
-        for copy in pre_x(h) + pre_z(h) + pre_y(h):
+        for copy in pre_z(h) + pre_y(h):
+            copy.start()
+        flip_x(h).wait_recv()
+        for copy in pre_x(h):
             copy.start()
 
     total = jnp.zeros((16, 512), F32)
@@ -306,11 +322,11 @@
     def pass_on(h):
         for copy in pre_x(h):
             copy.wait_recv()
-        for d in (1, 3, 2):
+        for d in (1, 3):
             last_x(h, d).start()
         for copy in pre_z(h) + pre_y(h):
             copy.wait_recv()
-        for d in (1, 3, 2):
+        for d in (1, 3):
             last_z(h, d).start()
             last_y(h, d).start()
         if h == 0:
@@ -321,15 +337,24 @@
         for group in range(3):
             share(h, group, 0).start()
 
+    def relay(h):
+        moves = relays(h)
+        for k, (group, d) in enumerate(((0, 1), (0, 3), (1, 1), (1, 3), (2, 3), (2, 1))):
+            lasts[group](h, d).wait_recv()
+            moves[k].start()
+            share(h, group, d if group == 2 else 4 - d).start()
+
     def hand_over(h):
-        for d in (1, 3, 2):
-            for group in (1, 0, 2):
-                lasts[group](h, d).wait_recv()
-                share(h, group, d if group == 2 else 4 - d).start()
-            if h == 0:
+        moves = relays(h)
+        for group in range(3):
+            moves[2 * group].wait_recv()
+            moves[2 * group + 1].wait_recv()
+            share(h, group, 2).start()
+        if h == 0:
+            for d in (1, 3, 2):
                 last_t(d).wait_recv()
                 share_t(4 - d).start()
-        for d in range(4):
+        for d in (0, 1, 3, 2):
             for group in range(3):
                 share(h, group, d).wait_recv()
             if h == 0:
@@ -358,7 +383,9 @@
     prepare(1)
     pass_on(1)
     prepare(2)
+    relay(0)
     prepare(3)
+    relay(1)
     hand_over(0)
     correlate(0)
     hand_over(1)
@@ -424,10 +451,10 @@
                     wb[16 - j, 1, pl.ds(c, 16), cols] = (-sp[j]).astype(BF16)
 
     for h in range(2):
-        for copy in pre_x(h) + pre_y(h) + pre_z(h):
+        for copy in [flip_x(h)] + pre_x(h) + pre_y(h) + pre_z(h) + relays(h):
             copy.wait_send()
         for group in range(3):
-            for d in (1, 2, 3):
+            for d in (1, 3):
                 lasts[group](h, d).wait_send()
             for d in range(4):
                 share(h, group, d).wait_send()
@@ -437,8 +464,18 @@
     for d in range(4):
         share_t(d).wait_send()
 
+    def choose(it, values):
+        out = values[0]
+        for k in range(1, 8):
+            out = jnp.where(it == k, values[k], out)
+        return out
+
+    def step_of(it):
+        return choose(it, (2, 1, 3, 2, 0, 1, 3, 0)), choose(it, (0, 0, 0, 1, 0, 1, 1, 1))
+
     def target(it):
-        return (x + 1 + it) % 4, it // 4
+        step, h = step_of(it)
+        return (x + step) % 4, h
 
     def trade(it):
         xt, h = target(it)
@@ -452,11 +489,24 @@
             for k, (src, dst) in enumerate(pairs)
         ]
 
-    def first_x(it):
+    def half_x(h, k):
+        return remote(
+            gx.at[e, k, :, (x + 2) % 4, h], qx.at[k, h], qx_s.at[k, h], qx_r.at[k, h],
+            at_x(1 + 2 * k),
+        )
+
+    def half_z(it, k):
         xt, h = target(it)
-        u = it % 4
+        zh_, zl_ = flip(2)
         return remote(
-            gx.at[e, :, :, xt, h], rx1.at[u, h], x1_s.at[u, h], x1_r.at[u, h], at_x(u + 1)
+            gz.at[e, zh_, pl.ds(2 * k, 2), zl_, h, xt], qz.at[k, it],
+            qz_s.at[k, it], qz_r.at[k, it], at_z(1 + 2 * k),
+        )
+
+    def first_x(h, k):
+        return remote(
+            gx.at[e, :, :, (x + 1 + 2 * k) % 4, h], rx1.at[k, h],
+            x1_s.at[k, h], x1_r.at[k, h], at_x(1 + 2 * k),
         )
 
     def first_y(it, d):
@@ -466,12 +516,12 @@
             y1_s.at[d - 1, it], y1_r.at[d - 1, it], at_y(d),
         )
 
-    def first_z(it, d):
+    def first_z(it, k):
         xt, h = target(it)
-        zh_, zl_ = flip(d)
+        zh_, zl_ = flip(1 + 2 * k)
         return remote(
-            gz.at[e, zh_, :, zl_, h, xt], rz1.at[d - 1, h, :, xt],
-            z1_s.at[d - 1, it], z1_r.at[d - 1, it], at_z(d),
+            gz.at[e, zh_, :, zl_, h, xt], rz1.at[k, h, :, xt],
+            z1_s.at[k, it], z1_r.at[k, it], at_z(1 + 2 * k),
         )
 
     def settle(it):
@@ -492,15 +542,36 @@
                 gz[e, w, v, :, h, xt].astype(F32) + cz[w, v, :, h, xt].astype(F32)
             ).astype(BF16)
 
-        @pl.when(it % 4 != 3)
+        @pl.when((it == 0) | (it == 3))
         def _():
-            first_x(it).start()
-
-        for d in (1, 3, 2):
-            first_z(it, d).start()
+            half_x(h, 0).start()
+            half_x(h, 1).start()
+
+        for k in range(2):
+            half_z(it, k).start()
+        for d in (1, 3, 2):
             first_y(it, d).start()
 
-    @pl.loop(0, 8)
+    def finish(it):
+        xt, h = target(it)
+        for k in range(2):
+            @pl.when((it == 1 + k) | (it == 5 + k))
+            def _(k=k):
+                half_x(h, k).wait_recv()
+                gx[e, k, :, xt, h] = (
+                    gx[e, k, :, xt, h].astype(F32) + qx[k, h].astype(F32)
+                ).astype(BF16)
+                first_x(h, k).start()
+
+        for k in range(2):
+            half_z(it, k).wait_recv()
+            zh_, zl_ = flip(3 - 2 * k)
+            at = pl.ds(2 * k, 2)
+            gz[e, zh_, at, zl_, h, xt] = (
+                gz[e, zh_, at, zl_, h, xt].astype(F32) + qz[k, it].astype(F32)
+            ).astype(BF16)
+            first_z(it, 1 - k).start()
+
     def accumulate(it):
         xt, h = target(it)
         for zv in range(2):
@@ -518,11 +589,19 @@
         for copy in trade(it):
             copy.start()
 
-        @pl.when(it > 0)
+    @pl.loop(0, 8 + FINISH)
+    def steps(it):
+        @pl.when(it < 8)
         def _():
-            settle(it - 1)
-
-    settle(7)
+            accumulate(it)
+
+        @pl.when((it >= SETTLE) & (it < 8 + SETTLE))
+        def _():
+            settle(it - SETTLE)
+
+        @pl.when(it >= FINISH)
+        def _():
+            finish(it - FINISH)
 
     def late(stage, group, h, d, src, dst, where):
         return remote(
@@ -557,39 +636,39 @@
         return acc
 
     for h in range(2):
-        for u in range(3):
-            first_x(u + 4 * h).wait_recv()
+        for k in range(2):
+            first_x(h, k).wait_recv()
 
         @pl.loop(0, 8)
         def add_x1(s, h=h):
             w, v = s // 4, s % 4
             gx[e, w, v, x, h] = total_of(
-                gx[e, w, v, x, h], [rx1[u, h, w, v] for u in range(3)]
+                gx[e, w, v, x, h], [rx1[k, h, w, v] for k in range(2)]
             ).astype(BF16)
 
         for d in (1, 3, 2):
             second_x(h, d).start()
-        for it in range(4 * h, 4 * h + 4):
-            for d in (1, 2, 3):
-                first_z(it, d).wait_recv()
+        for it in ((0, 1, 2, 4), (3, 5, 6, 7))[h]:
+            for k in range(2):
+                first_z(it, k).wait_recv()
 
         @pl.loop(0, 4)
         def add_z1(v, h=h):
             gz[e, zh, v, zl, h] = total_of(
-                gz[e, zh, v, zl, h], [rz1[d, h, v] for d in range(3)]
+                gz[e, zh, v, zl, h], [rz1[k, h, v] for k in range(2)]
             ).astype(BF16)
 
         for d in (1, 3, 2):
             second_z(h, d).start()
-        for it in range(4 * h, 4 * h + 4):
+        for it in ((0, 1, 2, 4), (3, 5, 6, 7))[h]:
             for d in (1, 2, 3):
                 first_y(it, d).wait_recv()
 
         @pl.loop(0, 8)
         def add_y1(s, h=h):
-            w, k = s // 4, s % 4
-            gy[e, w, y, h, k] = total_of(
-                gy[e, w, y, h, k], [ry1[d, h, w, k] for d in range(3)]
+            w, v = s // 4, s % 4
+            gy[e, w, y, h, v] = total_of(
+                gy[e, w, y, h, v], [ry1[d, h, w, v] for d in range(3)]
             ).astype(BF16)
 
         for d in (1, 3, 2):
@@ -636,15 +715,24 @@
     for it in range(8):
         for copy in trade(it):
             copy.wait_send()
-        if it % 4 != 3:
-            first_x(it).wait_send()
+        for k in range(2):
+            half_z(it, k).wait_send()
+            first_z(it, k).wait_send()
         for d in (1, 2, 3):
             first_y(it, d).wait_send()
-            first_z(it, d).wait_send()
+    for h in range(2):
+        for k in range(2):
+            half_x(h, k).wait_send()
+            first_x(h, k).wait_send()
     for copy in (second_x, second_y, second_z, third_x, third_y, third_z):
         for h in range(2):
             for d in (1, 2, 3):
                 copy(h, d).wait_send()
+
+
+def write(sums, prob, sums_out, prob_out):
+    sums_out[...] = sums[...]
+    prob_out[...] = prob[...]
 
 
 def on_device(spectra, offsets, groups, ctf, noise_weight, references):
@@ -677,9 +765,11 @@
             pltpu.VMEM((IMG, DEPTH), BF16),
             pltpu.VMEM((IMG, A), F32),
             pltpu.VMEM((R, IMG), F32),
-            pltpu.VMEM((3, 2, 2, 4, 2, 16, WX), BF16),
+            pltpu.VMEM((2, 2, 4, 2, 16, WX), BF16),
+            pltpu.VMEM((2, 8, 2, 16, WZ), BF16),
+            pltpu.VMEM((2, 2, 2, 4, 2, 16, WX), BF16),
             pltpu.VMEM((3, 2, 2, 4, 2, 16, WY), BF16),
-            pltpu.VMEM((3, 2, 4, 4, 16, WZ), BF16),
+            pltpu.VMEM((2, 2, 4, 4, 16, WZ), BF16),
             pltpu.VMEM((3, 2, 2, 2, 16, WX), BF16),
             pltpu.VMEM((3, 2, 4, 16, WY), BF16),
             pltpu.VMEM((3, 2, 4, 16, WZ), BF16),
@@ -691,12 +781,16 @@
             sem((2, 40)),
             sem((3, 8)),
             sem((3, 8)),
-            sem((3, 2)),
-            sem((3, 2)),
+            sem((2, 2)),
+            sem((2, 2)),
+            sem((2, 8)),
+            sem((2, 8)),
+            sem((2, 2)),
+            sem((2, 2)),
             sem((3, 8)),
             sem((3, 8)),
-            sem((3, 8)),
-            sem((3, 8)),
+            sem((2, 8)),
+            sem((2, 8)),
             sem((2, 3, 2, 3)),
             sem((2, 3, 2, 3)),
         ],
@@ -717,6 +811,16 @@
         references,
         jnp.asarray(harmonic_rows()),
     )
+    sums, prob = pl.pallas_call(
+        write,
+        out_shape=(
+            jax.ShapeDtypeStruct((16, 2048), F32),
+            jax.ShapeDtypeStruct((1, IMG), F32),
+        ),
+        in_specs=[vmem, vmem],
+        out_specs=(vmem, vmem),
+        name="write",
+    )(sums, prob)
     return sums, prob.reshape(-1)
 
 

time: 85.7 us -> 79.9 us (0.932)
  Pallas kernels: 82.1 us -> 79.1 us
  local copies, waits for them, and re-layouts: 2.8 us -> 0 us
    pallas_call x1, Pallas kernels: 82.1 us -> 77.5 us  [on_device(): pl.pallas_call(kernel, out_shape=(jax.ShapeDtypeStruct((16, 2048), F32),...]
    unnamed x2 -> x0, local copies, waits for them, and re-layouts: 2.8 us -> none
    pallas_call x0 -> x1, Pallas kernels: none -> 1.57 us  [on_device(): pl.pallas_call(write, out_shape=(jax.ShapeDtypeStruct((16, 2048), F32), j...]
where the time goes in v3:
time: 79.9 us; the launch traced here: 79.7 us
  Pallas kernels  79.1 us (99%)
    pallas_call x1, Pallas kernels, on_device(): pl.pallas_call(kernel, out_shape=(jax.ShapeDtypeStruct((16, 2048), F32),...  77.5 us

profile of v3, /device:TPU:0, one launch (start us, length us, event | category | flops | bytes accessed | tf_op | source)
XLA Modules:
  0.0 79.7 jit_solution(13428202568170766049)
XLA Ops:
  0.6 77.5 %classify.1 = (f32[16,2048]{1,0:T(8,128)}, f32[1,256]{1,0:T(1,128)}) custom-call(bf16[256,64,256]{2,1,0:T(8,128)(2,1)} %spectra.1, bf16[64,176,256]{2,1,0:T(8,128)(2,1)} %constant.4.clone.table, s32[2,256]{1,0:T(2,128)} %bitcast.4, s32[1,256]{1,0:T(1,128)} %bitcast.5, f32[32,64]{1,0:T(8,128)} %ctf.1, f32[1,64]{1,0:T(1,128)} %bitcast.7, ...), custom_call_target="tpu_custom_call" | custom-call | flops 15032385536 | bytes 25165824 | tf_op jit(solution)/shard_map/classify/pallas_call | solution.py:742
  78.1 1.6 %write.1 = (f32[16,2048]{1,0:T(8,128)}, f32[1,256]{1,0:T(1,128)}) custom-call(f32[16,2048]{1,0:T(8,128)} %get-tuple-element.6.sums, f32[1,256]{1,0:T(1,128)} %get-tuple-element.7.prob), custom_call_target="tpu_custom_call" | custom-call | tf_op jit(solution)/shard_map/write/pallas_call | solution.py:814

commit v4 on v3

--- a/solution.py
+++ b/solution.py
@@ -24,7 +24,7 @@
 DEPTH = 176
 WX, WY, WZ = 384, 256, 384
 
-SETTLE, FINISH = 3, 6
+SETTLE, FINISH = 2, 5
 
 S1 = math.sqrt(0.5)
 C1 = math.cos(math.pi / 8)
@@ -416,7 +416,7 @@
                 top = jnp.maximum(top, out[k])
             return top
 
-        top = lax.fori_loop(0, 32, scores, jnp.full((8, 128), -jnp.inf, F32))
+        top = lax.fori_loop(0, 32, scores, jnp.full((8, 128), -jnp.inf, F32), unroll=4)
         top = jnp.max(top, axis=0, keepdims=True)
 
         def exponents(b, total, top=top, at=at):
@@ -427,11 +427,11 @@
                 total = total + value
             return total
 
-        total = lax.fori_loop(0, 32, exponents, jnp.zeros((8, 128), F32))
+        total = lax.fori_loop(0, 32, exponents, jnp.zeros((8, 128), F32), unroll=8)
         scale = 1.0 / jnp.sum(total, axis=0, keepdims=True)
         prob_out[:, t * 128 : (t + 1) * 128] = scale
 
-        @pl.loop(0, 16)
+        @pl.loop(0, 16, unroll=2)
         def back(b, t=t, at=at, scale=scale):
             c = pl.multiple_of(b * 16, 16)
             p = [qb[pl.ds(at(k, c), 16), :] * scale for k in range(16)]

time: 79.9 us -> 78.1 us (0.977)
  Pallas kernels: 79.1 us -> 77.3 us
    pallas_call x1, Pallas kernels: 77.5 us -> 75.7 us  [on_device(): pl.pallas_call(kernel, out_shape=(jax.ShapeDtypeStruct((16, 2048), F32),...]
where the time goes in v4:
time: 78.1 us; the launch traced here: 77.9 us
  Pallas kernels  77.3 us (99%)
    pallas_call x1, Pallas kernels, on_device(): pl.pallas_call(kernel, out_shape=(jax.ShapeDtypeStruct((16, 2048), F32),...  75.7 us
    pallas_call x1, Pallas kernels, on_device(): pl.pallas_call(write, out_shape=(jax.ShapeDtypeStruct((16, 2048), F32), j...  1.57 us

profile of v4, /device:TPU:0, one launch (start us, length us, event | category | flops | bytes accessed | tf_op | source)
XLA Modules:
  0.0 77.9 jit_solution(15006628807526073237)
XLA Ops:
  0.6 75.7 %classify.1 = (f32[16,2048]{1,0:T(8,128)}, f32[1,256]{1,0:T(1,128)}) custom-call(bf16[256,64,256]{2,1,0:T(8,128)(2,1)} %spectra.1, bf16[64,176,256]{2,1,0:T(8,128)(2,1)} %constant.4.clone.table, s32[2,256]{1,0:T(2,128)} %bitcast.4, s32[1,256]{1,0:T(1,128)} %bitcast.5, f32[32,64]{1,0:T(8,128)} %ctf.1, f32[1,64]{1,0:T(1,128)} %bitcast.7, ...), custom_call_target="tpu_custom_call" | custom-call | flops 15032385536 | bytes 25165824 | tf_op jit(solution)/shard_map/classify/pallas_call | solution.py:742
  76.3 1.6 %write.1 = (f32[16,2048]{1,0:T(8,128)}, f32[1,256]{1,0:T(1,128)}) custom-call(f32[16,2048]{1,0:T(8,128)} %get-tuple-element.6.sums, f32[1,256]{1,0:T(1,128)} %get-tuple-element.7.prob), custom_call_target="tpu_custom_call" | custom-call | tf_op jit(solution)/shard_map/write/pallas_call | solution.py:814

commit v5 on v4

--- a/solution.py
+++ b/solution.py
@@ -361,7 +361,7 @@
                 share_t(d).wait_recv()
 
     def correlate(h):
-        @pl.loop(0, 4)
+        @pl.loop(0, 4, unroll=2)
         def _(k):
             for zv in range(2):
                 j = zv * 8 + k * 2 + h
@@ -529,7 +529,7 @@
         for copy in trade(it):
             copy.wait_recv()
 
-        @pl.loop(0, 8)
+        @pl.loop(0, 8, unroll=2)
         def add(s):
             w, v = s // 4, s % 4
             gx[e, w, v, xt, h] = (
@@ -639,7 +639,7 @@
         for k in range(2):
             first_x(h, k).wait_recv()
 
-        @pl.loop(0, 8)
+        @pl.loop(0, 8, unroll=4)
         def add_x1(s, h=h):
             w, v = s // 4, s % 4
             gx[e, w, v, x, h] = total_of(
@@ -652,7 +652,7 @@
             for k in range(2):
                 first_z(it, k).wait_recv()
 
-        @pl.loop(0, 4)
+        @pl.loop(0, 4, unroll=4)
         def add_z1(v, h=h):
             gz[e, zh, v, zl, h] = total_of(
                 gz[e, zh, v, zl, h], [rz1[k, h, v] for k in range(2)]
@@ -664,7 +664,7 @@
             for d in (1, 2, 3):
                 first_y(it, d).wait_recv()
 
-        @pl.loop(0, 8)
+        @pl.loop(0, 8, unroll=4)
         def add_y1(s, h=h):
             w, v = s // 4, s % 4
             gy[e, w, y, h, v] = total_of(

time: 78.1 us -> 77.1 us (0.987)
  Pallas kernels: 77.3 us -> 76.3 us
    pallas_call x1, Pallas kernels: 75.7 us -> 74.7 us  [on_device(): pl.pallas_call(kernel, out_shape=(jax.ShapeDtypeStruct((16, 2048), F32),...]
where the time goes in v5:
time: 77.1 us; the launch traced here: 76.9 us
  Pallas kernels  76.3 us (99%)
    pallas_call x1, Pallas kernels, on_device(): pl.pallas_call(kernel, out_shape=(jax.ShapeDtypeStruct((16, 2048), F32),...  74.7 us
    pallas_call x1, Pallas kernels, on_device(): pl.pallas_call(write, out_shape=(jax.ShapeDtypeStruct((16, 2048), F32), j...  1.57 us

profile of v5, /device:TPU:0, one launch (start us, length us, event | category | flops | bytes accessed | tf_op | source)
XLA Modules:
  0.0 76.9 jit_solution(11673265084875957844)
XLA Ops:
  0.6 74.7 %classify.1 = (f32[16,2048]{1,0:T(8,128)}, f32[1,256]{1,0:T(1,128)}) custom-call(bf16[256,64,256]{2,1,0:T(8,128)(2,1)} %spectra.1, bf16[64,176,256]{2,1,0:T(8,128)(2,1)} %constant.4.clone.table, s32[2,256]{1,0:T(2,128)} %bitcast.4, s32[1,256]{1,0:T(1,128)} %bitcast.5, f32[32,64]{1,0:T(8,128)} %ctf.1, f32[1,64]{1,0:T(1,128)} %bitcast.7, ...), custom_call_target="tpu_custom_call" | custom-call | flops 15032385536 | bytes 25165824 | tf_op jit(solution)/shard_map/classify/pallas_call | solution.py:742
  75.4 1.6 %write.1 = (f32[16,2048]{1,0:T(8,128)}, f32[1,256]{1,0:T(1,128)}) custom-call(f32[16,2048]{1,0:T(8,128)} %get-tuple-element.6.sums, f32[1,256]{1,0:T(1,128)} %get-tuple-element.7.prob), custom_call_target="tpu_custom_call" | custom-call | tf_op jit(solution)/shard_map/write/pallas_call | solution.py:814
